TPU v7x, 32 devices: a whole 2x2x4 slice. The times are simulated.
32 devices in a mesh: tex: 16 (over z, x, core), view: 2 (over y).
Axes of the slice: x: 2, y: 2, z: 4, core: 2. Of those that a mesh axis runs over, the one named last changes fastest.
Arguments:
- measured: bfloat16 [384, 160, 151], P('tex', 'view'), may hold values from -6 to 6
- view_mask: int32 [160], P('view'), may hold values from 0 to 1, as said below
- tex_factor: float32 [384, 256], P('tex'), may hold values from -6 to 6
- view_factor: float32 [160, 64], P('view'), as said below
- light_factor: bfloat16 [151, 64], replicated, as said below
- core_tensor: float32 [256, 64, 64], P('tex', 'view'), may hold values from -6 to 6
Outputs:
- tex_updated: float32 [384, 256], P('tex')
- view_updated: float32 [160, 64], P('view')
- core_updated: float32 [256, 64, 64], P('tex', 'view')
Inputs may be any that keep to these rules, and one draw needn't show every extreme that they name: `view_mask`: exactly 151 of the 160 entries are 1. `view_factor`: entries of order one. `light_factor`: entries of order one.
All inputs are finite; a program needn't handle non-finite values.
Results may differ from a plain program's by a relative error of at most 0.014.
Values may be sent and summed in bfloat16 or wider, within the bound.
A program may use at most 64 MiB of HBM per device.

v0:
```python
import jax
import jax.numpy as jnp
from jax import lax
from jax.sharding import PartitionSpec as P

RT = 256
RV = 64
RL = 64
VALID = 151
L = 151


def per_device(measured, view_mask, tex_factor, view_factor, light_factor, core_tensor):
    tex_count = lax.axis_size("tex")
    view_count = lax.axis_size("view")
    tex_rows = measured.shape[0]
    texels_all = tex_rows * tex_count
    band_width = RV // view_count
    band_start = lax.axis_index("view") * band_width
    scaling = (RT * RV * RL) ** (-0.5)
    rate_tex = RT / (VALID * L)
    rate_view = RV / (texels_all * L)
    rate_core = RT * RV * RL / (texels_all * VALID * L)
    weights = view_mask.astype(jnp.float32)[None, :, None]
    tex_now = tex_factor
    view_now = view_factor
    core_now = core_tensor
    tex_bf = tex_now.astype(jnp.bfloat16)
    view_bf = view_now.astype(jnp.bfloat16)
    core_bf = core_now.astype(jnp.bfloat16)
    core_band = lax.all_gather(core_bf, "view", axis=1, tiled=True)
    core_whole = lax.all_gather(core_band, "tex", axis=0, tiled=True)
    core_flat = core_whole.reshape(RT, RV * RL)
    projected = jnp.dot(tex_bf, core_flat, preferred_element_type=jnp.float32).astype(jnp.bfloat16)
    projected = projected.reshape(tex_rows, RV, RL)
    mixed = jnp.einsum(
        "vb,tbc->tvc", view_bf, projected, preferred_element_type=jnp.float32
    ).astype(jnp.bfloat16)
    approx = jnp.einsum("tvc,lc->tvl", mixed, light_factor, preferred_element_type=jnp.float32)
    resid = (weights * (scaling * approx - measured.astype(jnp.float32))).astype(jnp.bfloat16)
    back = jnp.einsum(
        "tvl,lc->tvc", resid, light_factor, preferred_element_type=jnp.float32
    ).astype(jnp.bfloat16)
    view_part = scaling * jnp.einsum(
        "tvc,tbc->vb", back, projected, preferred_element_type=jnp.float32
    )
    grad_view = lax.psum(view_part, "tex")
    partial_y = jnp.einsum("vb,tvc->tbc", view_bf, back, preferred_element_type=jnp.float32)
    summed = lax.psum_scatter(
        partial_y.astype(jnp.bfloat16), "view", scatter_dimension=1, tiled=True
    )
    core_slice = lax.dynamic_slice_in_dim(core_whole, band_start, band_width, 1)
    tex_part = scaling * lax.dot_general(
        summed.reshape(tex_rows, band_width * RL),
        core_slice.reshape(RT, band_width * RL),
        (((1,), (1,)), ((), ())),
        preferred_element_type=jnp.float32,
    )
    grad_tex = lax.psum(tex_part, "view")
    flat_split = summed.reshape(tex_rows, band_width * RL)
    grad_core = lax.psum_scatter(
        scaling
        * lax.dot_general(
            tex_bf, flat_split, (((0,), (0,)), ((), ())), preferred_element_type=jnp.float32
        ),
        "tex",
        scatter_dimension=0,
        tiled=True,
    )
    tex_now = tex_now - rate_tex * grad_tex
    view_now = view_now - rate_view * grad_view
    core_now = core_now - rate_core * grad_core.reshape(core_now.shape)
    return (tex_now, view_now, core_now)


def solution(mesh):
    return jax.shard_map(
        per_device,
        mesh=mesh,
        in_specs=(
            P("tex", "view", None),
            P("view"),
            P("tex", None),
            P("view", None),
            P(),
            P("tex", "view", None),
        ),
        out_specs=(P("tex", None), P("view", None), P("tex", "view", None)),
        check_vma=False,
    )
```

profile of v0, /device:TPU:0, one launch (start us, length us, event | category | flops | bytes accessed | tf_op | source)
XLA Modules:
  0.0 175.3 jit_solution(8369212737743914102)
XLA Ops:
  7.2 1.1 copy.43
  8.3 7.1 %all_gather.6 = bf16[16,64,64]{2,0,1:T(8,128)(2,1)S(1)} all-gather(bf16[16,32,64]{2,0,1:T(8,128)(2,1)S(1)} %copy.43), channel_id=1, replica_groups=mesh['tex'=16,'view'=2] {'view'}, dimensions={1}, use_global_device_ids=true | all-gather | bytes 196608 | tf_op jit(solution)/shard_map/all_gather | solution.py:31
  15.5 0.8 copy.27
  16.3 0.7 convert_element_type.36
  17.0 51.5 %all-gather.2.cloned.1.call-done = bf16[256,64,64]{2,1,0:T(8,128)(2,1)} async-done(((bf16[16,64,64]{2,1,0:T(8,128)(2,1)}), bf16[256,64,64]{2,1,0:T(8,128)(2,1)}) %all-gather.2.cloned.1.call-update) | async-done | bytes 2097168 | tf_op jit(solution)/shard_map/all_gather | solution.py:32
  68.5 4.9 %copy.28 = bf16[256,64,64]{0,2,1:T(8,128)(2,1)S(1)} copy(bf16[256,64,64]{2,1,0:T(8,128)(2,1)} %all-gather.2.cloned.1.call-done) | data formatting | bytes 4194304 | tf_op jit(solution)/shard_map/all_gather | solution.py:32
  73.4 0.6 convolution_convert_fusion
  74.1 0.4 reshape.22
  74.5 0.3 fusion.3
  74.8 1.8 %fusion.2 = bf16[24,80,64]{1,2,0:T(8,128)(2,1)S(1)} fusion(bf16[24,80,64]{1,2,0:T(8,128)(2,1)S(1)} %fusion.3, bf16[24,80,151]{1,0,2:T(8,128)(2,1)} %param.6, f32[80]{0:T(128)S(1)} %convert_element_type.36, bf16[151,64]{0,1:T(8,128)(2,1)S(1)} %copy-done), kind=kOutput, calls=%fused_computation.5 | convolution fusion | flops 75792000 | bytes 1091008 | tf_op jit(solution)/shard_map/tvl,lc->tvc/dot_general | solution.py:41
  76.9 1.0 copy.31
  77.9 11.7 %reduce-scatter.5.cloned.1.call-done = bf16[24,32,64]{2,0,1:T(8,128)(2,1)} async-done(((bf16[24,64,64]{2,0,1:T(8,128)(2,1)}), bf16[24,32,64]{2,0,1:T(8,128)(2,1)}) %reduce-scatter.5.cloned.1.call-update) | async-done | bytes 98320 | tf_op jit(solution)/shard_map/reduce_scatter | solution.py:49
  89.6 1.0 copy.33
  90.8 1.8 %fusion = f32[256,2048]{0,1:T(8,128)} fusion(bf16[24,2048]{1,0:T(8,128)(2,1)S(1)} %reshape.23, f32[24,256]{1,0:T(8,128)S(1)} %copy-done.4), kind=kOutput, calls=%fused_computation.2 | convolution fusion | flops 25696256 | bytes 2220032 | tf_op jit(solution)/shard_map/dot_general | solution.py:63
  92.6 2.9 %copy.36 = f32[256,2048]{1,0:T(8,128)} copy(f32[256,2048]{0,1:T(8,128)} %fusion) | data formatting | bytes 4194304
  95.6 0.3 fusion.5
  95.9 61.3 %psum.15 = f32[80,64]{0,1:T(8,128)S(1)} all-reduce(f32[80,64]{0,1:T(8,128)S(1)} %fusion.5), channel_id=1, replica_groups=mesh['tex'=16,'view'=2] {'tex'}, use_global_device_ids=true, to_apply=%region_2.0 | all-reduce | flops 5120 | bytes 40960 | tf_op jit(solution)/shard_map/psum | solution.py:47
  157.2 0.6 multiply_subtract_fusion
  157.8 0.3 fusion.6
  158.1 7.5 %psum.14 = f32[24,256]{1,0:T(8,128)S(1)} all-reduce(f32[24,256]{1,0:T(8,128)S(1)} %fusion.6), channel_id=1, replica_groups=mesh['tex'=16,'view'=2] {'view'}, use_global_device_ids=true, to_apply=%region_1.0 | all-reduce | flops 6144 | bytes 49152 | tf_op jit(solution)/shard_map/psum | solution.py:59
  165.6 0.6 multiply_subtract_fusion.1
  166.3 1.3 copy.37
  167.6 0.4 copy.34
  168.0 0.7 sub.15
  (20 shorter events, 0.8 us)
Async XLA Ops:
  7.2 67.6 %copy-start = (bf16[151,64]{0,1:T(8,128)(2,1)S(1)}, bf16[151,64]{0,1:T(8,128)(2,1)}, u32[]{:S(2)}) copy-start(bf16[151,64]{0,1:T(8,128)(2,1)} %param.10) | copy-start | bytes 57988
  7.2 61.3 %all-gather.2.cloned.1.call-start = ((), (), s32[]{:S(2)}) async-start(), calls=%async_computation.2 | async-start | bytes 4456448 | tf_op jit(solution)/shard_map/all_gather | solution.py:32
  16.3 73.4 %reduce-scatter.5.cloned.1.call-start = ((), (), s32[]{:S(2)}) async-start(), calls=%async_computation.3 | async-start | bytes 589824 | tf_op jit(solution)/shard_map/reduce_scatter | solution.py:49
  17.0 56.4 %copy-start.4 = (f32[24,256]{1,0:T(8,128)S(1)}, f32[24,256]{1,0:T(8,128)}, u32[]{:S(2)}) copy-start(f32[24,256]{1,0:T(8,128)} %param.8) | copy-start | bytes 73732
  73.4 1.1 copy-start.3
  77.9 88.4 %reduce-scatter.7.cloned.1.call-start = ((), (), s32[]{:S(2)}) async-start(), calls=%async_computation.4 | async-start | bytes 2228224
  95.6 62.3 %copy-start.2 = (bf16[24,32,64]{2,0,1:T(8,128)(2,1)S(1)}, bf16[24,32,64]{2,0,1:T(8,128)(2,1)}, u32[]{:S(2)}) copy-start(bf16[24,32,64]{2,0,1:T(8,128)(2,1)} %reduce-scatter.5.cloned.1.call-done) | copy-start | bytes 294916
  166.3 1.8 %copy-start.1 = (f32[16,32,64]{2,1,0:T(8,128)S(1)}, f32[16,32,64]{2,1,0:T(8,128)}, u32[]{:S(2)}) copy-start(f32[16,32,64]{2,1,0:T(8,128)} %param.11) | copy-start | bytes 393220
Sparse Core Ops, SparseCore 0:
  16.4 52.0 all-gather.1
  78.0 11.5 reduce-scatter.4
  95.7 61.6 reduce-scatter.6
where the time goes:
time: 176 us; the launch traced here: 175 us
  blocking collectives  76 us (43%)
  waiting for transfers between devices  63.3 us (36%)
  local copies, waits for them, and re-layouts  14 us (8%)
  between operations  13.9 us (8%)
  matrix products  5.36 us (3%)
  other arithmetic  2.73 us (2%)
    psum x1, blocking collectives, per_device(): grad_view = lax.psum(view_part, 'tex')  61.3 us
    all_gather x1, waiting for transfers between devices, per_device(): core_whole = lax.all_gather(core_band, 'tex', axis=0, tiled=True)  51.5 us
    reduce_scatter x1, waiting for transfers between devices, per_device(): lax.psum_scatter(partial_y.astype(jnp.bfloat16), 'view', scatter_dimensio...  11.7 us
    psum x1, blocking collectives, per_device(): grad_tex = lax.psum(tex_part, 'view')  7.53 us
    all_gather x1, blocking collectives, per_device(): core_band = lax.all_gather(core_bf, 'view', axis=1, tiled=True)  7.12 us
    unnamed x13, local copies, waits for them, and re-layouts  5.34 us
    all_gather x1, local copies, waits for them, and re-layouts, per_device(): core_whole = lax.all_gather(core_band, 'tex', axis=0, tiled=True)  4.92 us
  transfers between devices with their start and end apart: 3, of which 2 were waited for; matrix products, arithmetic and copies ran while one was open for 1% of the time, Pallas kernels for 0%

commit v1 on v0

v1 whole, which is shorter than its diff:
```python
import functools

import jax
import jax.numpy as jnp
from jax import lax
from jax.experimental import pallas as pl
from jax.experimental.pallas import tpu as pltpu
from jax.sharding import PartitionSpec as P

RT = 256
RV = 64
RL = 64
VALID = 151
L = 151
LINE = 4
GROUP = 256 // RL
LIGHTS = 256 * (-(-L // 256))
SCALING = (RT * RV * RL) ** (-0.5)
MESH = pl.DeviceIdType.MESH
BF = jnp.bfloat16
F32 = jnp.float32
NT = (((1,), (1,)), ((), ()))
TN = (((0,), (0,)), ((), ()))


def kernel(
    tex_count, view_count,
    g_ref, u_ref, v_ref, mask_ref, light_ref, meas_hbm,
    gu_ref, gv_ref, gg_ref,
    gbuf, meas, bdw, rbuf, p3, pall, ysend, yrecv, ysum, yflat,
    us, ur, gvs, gvr, rs, rc, xr, zr,
    meas_sem, ga_s, gb_s, gc_s, g_r, p_s, p_r, y_s, y_r, u_s, u_r, gv_s, gv_r,
    c_s, c_r, x_s, x_r, z_s, z_r,
):
    na = LINE
    nb = tex_count // (2 * na)
    me = lax.axis_index("tex")
    view = lax.axis_index("view")
    core = lax.rem(me, 2)
    b = lax.rem(me // 2, nb)
    a = me // (2 * nb)
    rows, width = g_ref.shape
    band = width // RL
    texels = u_ref.shape[0]
    groups = texels // GROUP
    steps = tex_count.bit_length() - 1

    def slot(ai, bi, ci):
        return (ai * nb + bi) * 2 + ci

    def push(src, dst, ssem, rsem, tex, vw):
        copy = pltpu.make_async_remote_copy(
            src_ref=src, dst_ref=dst, send_sem=ssem, recv_sem=rsem,
            device_id=(tex, vw), device_id_type=MESH,
        )
        copy.start()
        return copy

    def arrived(ref, sem):
        pltpu.make_async_copy(ref, ref, sem).wait()

    sibling = slot(a, b, 1 - core)
    pending = []

    for d in range(1, na):
        pending.append(push(g_ref, gbuf.at[me], ga_s.at[d - 1], g_r.at[me],
                            slot(lax.rem(a + d, na), b, core), view))
    for e in range(1, nb):
        pending.append(push(g_ref, gbuf.at[me], gb_s.at[0, e - 1], g_r.at[me],
                            slot(a, lax.rem(b + e, nb), core), view))
    pending.append(push(g_ref, gbuf.at[me], gc_s.at[0, 0], g_r.at[me], sibling, view))
    meas_copy = pltpu.make_async_copy(meas_hbm, meas, meas_sem)
    meas_copy.start()
    gbuf[me] = g_ref[...]

    bdw[...] = jnp.zeros_like(bdw)
    rbuf[...] = jnp.zeros_like(rbuf)
    for j in range(GROUP):
        bdw[j * LIGHTS:j * LIGHTS + L, j * RL:(j + 1) * RL] = light_ref[...]

    def across(d):
        ad = lax.rem(a + na - d, na)
        for e in range(1, nb):
            s = slot(ad, lax.rem(b + nb - e, nb), core)
            arrived(gbuf.at[s], g_r.at[s])
            pending.append(push(gbuf.at[s], gbuf.at[s], gc_s.at[d, e], g_r.at[s], sibling, view))

    for d in range(1, na):
        s = slot(lax.rem(a + na - d, na), b, core)
        arrived(gbuf.at[s], g_r.at[s])
        for e in range(1, nb):
            pending.append(push(gbuf.at[s], gbuf.at[s], gb_s.at[d, e - 1], g_r.at[s],
                                slot(a, lax.rem(b + e, nb), core), view))
        pending.append(push(gbuf.at[s], gbuf.at[s], gc_s.at[d, 0], g_r.at[s], sibling, view))
        across(d - 1)
    across(na - 1)
    for ai in range(na):
        for bi in range(nb):
            s = slot(ai, bi, 1 - core)
            arrived(gbuf.at[s], g_r.at[s])

    u_bf = u_ref[...].astype(BF)
    v_bf = v_ref[...].astype(BF)
    if rows % 16 == 0:
        g_all = gbuf[...].reshape(tex_count * rows, width)
    else:
        g_all = jnp.concatenate(
            [gbuf[j].astype(F32) for j in range(tex_count)], axis=0).astype(BF)

    proj = jnp.dot(u_bf, g_all, preferred_element_type=F32)
    for j in range(band):
        p3[j] = proj[:, j * RL:(j + 1) * RL]
    for t in range(0, texels, 2):
        pair = jnp.concatenate([p3[:, t, :], p3[:, t + 1, :]], axis=1)
        pall[view, :, t * RL:(t + 2) * RL] = pair.astype(BF)
    for w in range(1, view_count):
        pending.append(push(pall.at[view], pall.at[view], p_s.at[w - 1], p_r.at[view],
                            me, lax.rem(view + w, view_count)))
    meas_copy.wait()
    weights = mask_ref[...].astype(F32)
    for w in range(1, view_count):
        other = lax.rem(view + w, view_count)
        arrived(pall.at[other], p_r.at[other])

    gv = jnp.zeros(gv_ref.shape, F32)
    for k in range(groups):
        lanes = slice(k * GROUP * RL, (k + 1) * GROUP * RL)
        if band % 16 == 0:
            p4 = jnp.concatenate([pall[w, :, lanes] for w in range(view_count)], axis=0)
        else:
            p4 = jnp.concatenate(
                [pall[w, :, lanes].astype(F32) for w in range(view_count)], axis=0).astype(BF)
        q4 = jnp.dot(v_bf, p4, preferred_element_type=F32).astype(BF)
        a4 = lax.dot_general(q4, bdw[...], NT, preferred_element_type=F32)
        for j in range(GROUP):
            part = a4[:, j * LIGHTS:j * LIGHTS + L]
            resid = weights * (SCALING * part - meas[k * GROUP + j].astype(F32))
            rbuf[k, :, j * LIGHTS:j * LIGHTS + L] = resid.astype(BF)
        s4 = jnp.dot(rbuf[k], bdw[...], preferred_element_type=F32).astype(BF)
        gv = gv + lax.dot_general(s4, p4, NT, preferred_element_type=F32)
        y4 = lax.dot_general(v_bf, s4, TN, preferred_element_type=F32)
        for w in range(view_count):
            ysend[w, :, lanes] = y4[w * band:(w + 1) * band].astype(BF)

    for w in range(1, view_count):
        other = lax.rem(view + w, view_count)
        pending.append(push(ysend.at[other], yrecv.at[w - 1], y_s.at[w - 1], y_r.at[w - 1],
                            me, other))

    def gv_start(i, value):
        gvs[i] = value
        partner = me + (1 << i) - 2 * (1 << i) * lax.rem(me // (1 << i), 2)
        pending.append(push(gvs.at[i], gvr.at[i], gv_s.at[i], gv_r.at[i], partner, view))

    def gv_next(i):
        arrived(gvr.at[i], gv_r.at[i])
        value = gvs[i] + gvr[i]
        if i + 1 < steps:
            gv_start(i + 1, value)
        else:
            gv_ref[...] = value

    gv_start(0, SCALING * gv)

    for w in range(1, view_count):
        arrived(yrecv.at[w - 1], y_r.at[w - 1])
    total = ysend[view].astype(F32)
    for w in range(1, view_count):
        total = total + yrecv[w - 1].astype(F32)
    for t in range(texels):
        ysum[:, t, :] = total[:, t * RL:(t + 1) * RL]
    for j in range(0, band, 2):
        pair = jnp.concatenate([ysum[j], ysum[j + 1]], axis=1)
        yflat[:, j * RL:(j + 2) * RL] = pair.astype(BF)
    gv_next(0)

    y_bf = yflat[...]
    grad = SCALING * lax.dot_general(u_bf, y_bf, TN, preferred_element_type=F32)
    for j in range(tex_count):
        rs[j] = grad[j * rows:(j + 1) * rows].astype(BF)

    order = [d % na for d in range(1, na + 1)]
    for e in list(range(1, nb)) + [0]:
        for d in order:
            ad, be = lax.rem(a + d, na), lax.rem(b + e, nb)
            pending.append(push(rs.at[slot(ad, be, 1 - core)], rc.at[d, e], c_s.at[d, e], c_r.at[d, e],
                                sibling, view))

    us[...] = SCALING * lax.dot_general(y_bf, g_all, NT, preferred_element_type=F32)
    for w in range(1, view_count):
        pending.append(push(us, ur.at[w - 1], u_s.at[w - 1], u_r.at[w - 1],
                            me, lax.rem(view + w, view_count)))
    if steps > 1:
        gv_next(1)

    for e in range(1, nb):
        for d in order:
            ad, be = lax.rem(a + d, na), lax.rem(b + e, nb)
            s = slot(ad, be, core)
            arrived(rc.at[d, e], c_r.at[d, e])
            rs[s] = (rs[s].astype(F32) + rc[d, e].astype(F32)).astype(BF)
            pending.append(push(rs.at[s], xr.at[d, e - 1], x_s.at[d, e - 1], x_r.at[d, e - 1],
                                slot(a, be, core), view))
    if steps > 2:
        gv_next(2)
    for d in order:
        s = slot(lax.rem(a + d, na), b, core)
        arrived(rc.at[d, 0], c_r.at[d, 0])
        block = rs[s].astype(F32) + rc[d, 0].astype(F32)
        for e in range(1, nb):
            arrived(xr.at[d, e - 1], x_r.at[d, e - 1])
            block = block + xr[d, e - 1].astype(F32)
        if d:
            rs[s] = block.astype(BF)
            pending.append(push(rs.at[s], zr.at[d - 1], z_s.at[d - 1], z_r.at[d - 1],
                                slot(lax.rem(a + d, na), b, core), view))
    for i in range(3, steps):
        gv_next(i)

    total_u = us[...]
    for w in range(1, view_count):
        arrived(ur.at[w - 1], u_r.at[w - 1])
        total_u = total_u + ur[w - 1]
    gu_ref[...] = total_u
    for d in range(1, na):
        arrived(zr.at[d - 1], z_r.at[d - 1])
        block = block + zr[d - 1].astype(F32)
    gg_ref[...] = block
    for copy in pending:
        copy.wait_send()


def per_device(measured, view_mask, tex_factor, view_factor, light_factor, core_tensor):
    tex_count = lax.axis_size("tex")
    view_count = lax.axis_size("view")
    texels, views, _ = measured.shape
    rows, band, _ = core_tensor.shape
    width = band * RL
    texels_all = texels * tex_count
    nb = tex_count // (2 * LINE)
    steps = tex_count.bit_length() - 1
    peers = max(view_count - 1, 1)
    rate_tex = RT / (VALID * L)
    rate_view = RV / (texels_all * L)
    rate_core = RT * RV * RL / (texels_all * VALID * L)
    vmem = pl.BlockSpec(memory_space=pltpu.VMEM)
    dma = pltpu.SemaphoreType.DMA
    gu, gv, gg = pl.pallas_call(
        functools.partial(kernel, tex_count, view_count),
        out_shape=(
            jax.ShapeDtypeStruct((texels, RT), F32),
            jax.ShapeDtypeStruct((views, RV), F32),
            jax.ShapeDtypeStruct((rows, width), F32),
        ),
        in_specs=[vmem] * 5 + [pl.BlockSpec(memory_space=pl.ANY)],
        out_specs=(vmem, vmem, vmem),
        scratch_shapes=[
            pltpu.VMEM((tex_count, rows, width), BF),
            pltpu.VMEM((texels, views, L), BF),
            pltpu.VMEM((GROUP * LIGHTS, GROUP * RL), BF),
            pltpu.VMEM((texels // GROUP, views, GROUP * LIGHTS), BF),
            pltpu.VMEM((band, texels, RL), F32),
            pltpu.VMEM((view_count, band, texels * RL), BF),
            pltpu.VMEM((view_count, band, texels * RL), BF),
            pltpu.VMEM((peers, band, texels * RL), BF),
            pltpu.VMEM((band, texels, RL), F32),
            pltpu.VMEM((texels, width), BF),
            pltpu.VMEM((texels, RT), F32),
            pltpu.VMEM((peers, texels, RT), F32),
            pltpu.VMEM((steps, views, RV), F32),
            pltpu.VMEM((steps, views, RV), F32),
            pltpu.VMEM((tex_count, rows, width), BF),
            pltpu.VMEM((LINE, nb, rows, width), BF),
            pltpu.VMEM((LINE, max(nb - 1, 1), rows, width), BF),
            pltpu.VMEM((LINE - 1, rows, width), BF),
            dma, dma((LINE - 1,)), dma((LINE, max(nb - 1, 1))), dma((LINE, nb)), dma((tex_count,)),
            dma((peers,)), dma((view_count,)), dma((peers,)), dma((peers,)),
            dma((peers,)), dma((peers,)), dma((steps,)), dma((steps,)),
            dma((LINE, nb)), dma((LINE, nb)),
            dma((LINE, max(nb - 1, 1))), dma((LINE, max(nb - 1, 1))),
            dma((LINE - 1,)), dma((LINE - 1,)),
        ],
        compiler_params=pltpu.CompilerParams(
            has_side_effects=True, vmem_limit_bytes=48 * 1024 * 1024),
        cost_estimate=pl.CostEstimate(flops=10**9, bytes_accessed=10**7, transcendentals=0),
    )(core_tensor.astype(BF).reshape(rows, width), tex_factor, view_factor,
      view_mask.reshape(views, 1), light_factor, measured)
    return (
        tex_factor - rate_tex * gu,
        view_factor - rate_view * gv,
        core_tensor - rate_core * gg.reshape(core_tensor.shape),
    )


def solution(mesh):
    return jax.shard_map(
        per_device,
        mesh=mesh,
        in_specs=(
            P("tex", "view", None),
            P("view"),
            P("tex", None),
            P("view", None),
            P(),
            P("tex", "view", None),
        ),
        out_specs=(P("tex", None), P("view", None), P("tex", "view", None)),
        check_vma=False,
    )
```

time: 176 us -> 57.9 us (0.33)
  blocking collectives: 76 us -> 0 us
  waiting for transfers between devices: 63.3 us -> 0 us
  Pallas kernels: 0 us -> 48.7 us
  between operations: 13.9 us -> 0.71 us
  local copies, waits for them, and re-layouts: 14 us -> 5.93 us
  matrix products: 5.36 us -> 0 us
    psum x2 -> x0, blocking collectives: 68.9 us -> none  [the longest x1 61.3 us: per_device(): grad_view = lax.psum(view_part, 'tex')]
    all_gather x1 -> x0, waiting for transfers between devices: 51.5 us -> none  [per_device(): core_whole = lax.all_gather(core_band, 'tex', axis=0, tiled=True)]
    pallas_call x0 -> x1, Pallas kernels: none -> 48.7 us  [per_device(): pl.pallas_call(functools.partial(kernel, tex_count, view_count), out_shap...]
    reduce_scatter x1 -> x0, waiting for transfers between devices: 11.7 us -> none  [per_device(): lax.psum_scatter(partial_y.astype(jnp.bfloat16), 'view', scatter_dimensio...]
    all_gather x1 -> x0, blocking collectives: 7.12 us -> none  [per_device(): core_band = lax.all_gather(core_bf, 'view', axis=1, tiled=True)]
    all_gather x2 -> x0, local copies, waits for them, and re-layouts: 5.7 us -> none  [the longest x1 4.92 us: per_device(): core_whole = lax.all_gather(core_band, 'tex', axis=0, tiled=True)]
    dot_general x7 -> x0, matrix products: 5.36 us -> none  [the longest x1 1.82 us: per_device(): jnp.einsum('tvl,lc->tvc', resid, light_factor, preferred_element_type=jnp...]
    unnamed x13 -> x12, local copies, waits for them, and re-layouts: 5.34 us -> 5.55 us
  transfers between devices with their start and end apart: 3 -> 0, of which waited for: 2 -> 0; matrix products, arithmetic and copies ran while one was open for 1% -> 0% of each run, Pallas kernels for 0% -> 0%
where the time goes in v1:
time: 57.9 us; the launch traced here: 57.7 us
  Pallas kernels  48.7 us (84%)
  local copies, waits for them, and re-layouts  5.93 us (10%)
  other arithmetic  2.34 us (4%)
  between operations  0.71 us (1%)
    pallas_call x1, Pallas kernels, per_device(): pl.pallas_call(functools.partial(kernel, tex_count, view_count), out_shap...  48.7 us
    unnamed x12, local copies, waits for them, and re-layouts  5.55 us

profile of v1, /device:TPU:0, one launch (start us, length us, event | category | flops | bytes accessed | tf_op | source)
XLA Modules:
  0.0 57.7 jit_solution(17453503510323207404)
XLA Ops:
  0.6 0.0 copy-start.2
  0.6 0.9 %copy.11.light_ref = bf16[151,64]{1,0:T(8,128)(2,1)S(1)} copy(bf16[151,64]{0,1:T(8,128)(2,1)} %param.10) | data formatting | bytes 38656 | tf_op args[4]
  1.5 0.0 copy-done.2
  1.5 0.0 copy-start.3
  1.5 0.1 copy.9.v_ref
  1.6 0.6 copy-done.3
  2.2 0.1 copy.10.mask_ref
  2.3 1.0 %convert_element_type.3 = bf16[16,32,64]{2,1,0:T(8,128)(2,1)S(1)} convert(f32[16,32,64]{2,1,0:T(8,128)} %param.11) | non-fusion elementwise | flops 32768 | bytes 196608 | tf_op jit(solution)/shard_map/convert_element_type | solution.py:286
  3.3 0.2 reshape.15.g_ref
  3.4 0.0 copy-start
  3.5 2.5 %copy.12.meas_hbm = bf16[24,80,151]{2,1,0:T(8,128)(2,1)S(1)} copy(bf16[24,80,151]{1,0,2:T(8,128)(2,1)} %param.6) | data formatting | bytes 1159680 | tf_op args[0]
  6.0 0.0 copy-done
  6.0 48.7 %shard_map.85 = (f32[24,256]{1,0:T(8,128)S(1)}, f32[80,64]{1,0:T(8,128)S(1)}, f32[16,2048]{1,0:T(8,128)S(1)}) custom-call(bf16[16,2048]{1,0:T(8,128)(2,1)S(1)} %reshape.15.g_ref, f32[24,256]{1,0:T(8,128)S(1)} %copy-done, f32[80,64]{1,0:T(8,128)S(1)} %copy.9.v_ref, s32[80,1]{1,0:T(8,128)S(1)} %copy.10.mask_ref, bf16[151,64]{1,0:T(8,128)(2,1)S(1)} %copy.11.light_ref, ...), custom_call_target="tpu_custom_call" | custom-call | flops 1000000000 | bytes 10000000 | tf_op jit(solution)/shard_map/pallas_call | solution.py:248
  54.6 0.6 %multiply_subtract_fusion.1 = f32[24,256]{1,0:T(8,128)} fusion(f32[24,256]{1,0:T(8,128)S(1)} %copy-done, f32[24,256]{1,0:T(8,128)S(1)} %get-tuple-element.6), kind=kLoop, calls=%fused_computation.2 | loop fusion | flops 12288 | bytes 73728 | tf_op jit(solution)/shard_map/sub | solution.py:289
  55.3 0.7 %copy.14 = f32[80,64]{0,1:T(8,128)} copy(f32[80,64]{1,0:T(8,128)S(1)} %multiply_subtract_fusion) | data formatting | bytes 40960
  56.0 0.0 copy-start.1
  56.0 0.1 mul.27
  56.1 0.8 %copy-done.1 = f32[16,32,64]{2,1,0:T(8,128)S(1)} copy-done((f32[16,32,64]{2,1,0:T(8,128)S(1)}, f32[16,32,64]{2,1,0:T(8,128)}, u32[]{:S(2)}) %copy-start.1) | copy-done | bytes 131096
  56.9 0.7 %sub.11 = f32[16,32,64]{2,1,0:T(8,128)} subtract(f32[16,32,64]{2,1,0:T(8,128)S(1)} %copy-done.1, f32[16,32,64]{2,1,0:T(8,128)S(1)} %mul.27) | non-fusion elementwise | flops 32768 | bytes 393216 | tf_op jit(solution)/shard_map/sub | solution.py:291
  (2 shorter events, 0.0 us)
Async XLA Ops:
  0.6 0.9 %copy-start.2 = (f32[80,64]{0,1:T(8,128)S(1)}, f32[80,64]{0,1:T(8,128)}, u32[]{:S(2)}) copy-start(f32[80,64]{0,1:T(8,128)} %param.9) | copy-start | bytes 61444
  1.5 0.7 %copy-start.3 = (s32[80]{0:T(128)S(1)}, s32[80]{0:T(128)}, u32[]{:S(2)}) copy-start(s32[80]{0:T(128)} %param.7) | copy-start | bytes 964
  3.4 2.5 %copy-start = (f32[24,256]{1,0:T(8,128)S(1)}, f32[24,256]{1,0:T(8,128)}, u32[]{:S(2)}) copy-start(f32[24,256]{1,0:T(8,128)} %u_ref.1) | copy-start | bytes 73732
  56.0 0.9 %copy-start.1 = (f32[16,32,64]{2,1,0:T(8,128)S(1)}, f32[16,32,64]{2,1,0:T(8,128)}, u32[]{:S(2)}) copy-start(f32[16,32,64]{2,1,0:T(8,128)} %param.11) | copy-start | bytes 393220

commit v2 on v0

v2 whole, which is shorter than its diff:
```python
import functools

import jax
import jax.numpy as jnp
from jax import lax
from jax.experimental import pallas as pl
from jax.experimental.pallas import tpu as pltpu
from jax.sharding import PartitionSpec as P

RT = 256
RV = 64
RL = 64
VALID = 151
L = 151
LINE = 4
CHUNKS = 2
GROUP = 256 // RL
LIGHTS = 256 * (-(-L // 256))
SCALING = (RT * RV * RL) ** (-0.5)
MESH = pl.DeviceIdType.MESH
BF = jnp.bfloat16
F32 = jnp.float32
NT = (((1,), (1,)), ((), ()))
TN = (((0,), (0,)), ((), ()))


def kernel(
    tex_count, view_count, rates,
    core_ref, u_ref, vt_ref, mask_ref, lightt_ref, meas_hbm,
    u_out, vt_out, core_out,
    gl, gbuf, meas, mwide, mturn, weights, vcol, vrow, bdw, qbuf, rbuf, p3, pall,
    ysend, yrecv, ysum, yflat, us, ur, gvs, gvr, rs, rc, xr, zr,
    meas_sem, ga_s, gb_s, gc_s, g_r, p_s, p_r, y_s, y_r, u_s, u_r, gv_s, gv_r,
    c_s, c_r, x_s, x_r, z_s, z_r,
):
    na = LINE
    nb = tex_count // (2 * na)
    me = lax.axis_index("tex")
    view = lax.axis_index("view")
    core = lax.rem(me, 2)
    b = lax.rem(me // 2, nb)
    a = me // (2 * nb)
    rows, band, _ = core_ref.shape
    part = band // CHUNKS
    texels = u_ref.shape[0]
    views = vt_ref.shape[1]
    padded = vcol.shape[0]
    groups = texels // GROUP
    steps = tex_count.bit_length() - 1
    rate_tex, rate_view, rate_core = rates

    def slot(ai, bi, ci):
        return (ai * nb + bi) * 2 + ci

    def ahead(d):
        return lax.rem(a + d, na)

    def beside(e):
        return lax.rem(b + e, nb)

    def other(w):
        return lax.rem(view + w, view_count)

    sibling = slot(a, b, 1 - core)
    pending = []

    def push(src, dst, ssem, rsem, tex, vw):
        copy = pltpu.make_async_remote_copy(
            src_ref=src, dst_ref=dst, send_sem=ssem, recv_sem=rsem,
            device_id=(tex, vw), device_id_type=MESH,
        )
        copy.start()
        pending.append(copy)

    def arrived(ref, sem):
        pltpu.make_async_copy(ref, ref, sem).wait()

    barrier = pltpu.get_barrier_semaphore()
    peers = [(slot(ahead(d), b, core), view) for d in range(1, na)]
    peers += [(slot(a, beside(e), core), view) for e in range(1, nb)]
    peers += [(sibling, view)]
    peers += [(me, other(w)) for w in range(1, view_count)]
    for peer in peers:
        pl.semaphore_signal(barrier, inc=1, device_id=peer, device_id_type=MESH)
    meas_copy = pltpu.make_async_copy(meas_hbm, meas, meas_sem)
    meas_copy.start()
    for i in range(0, band, 2):
        pair = jnp.concatenate([core_ref[:, i, :], core_ref[:, i + 1, :]], axis=1).astype(BF)
        h, o = divmod(i, part)
        gl[h, :, o * RL:(o + 2) * RL] = pair
    pl.semaphore_wait(barrier, len(peers))

    for h in range(CHUNKS):
        for e in range(1, nb):
            push(gl.at[h], gbuf.at[h, me], gb_s.at[h, 0, e - 1], g_r.at[h, me],
                 slot(a, beside(e), core), view)
        for d in range(1, na):
            push(gl.at[h], gbuf.at[h, me], ga_s.at[h, d - 1], g_r.at[h, me],
                 slot(ahead(d), b, core), view)
        push(gl.at[h], gbuf.at[h, me], gc_s.at[h, 0, 0], g_r.at[h, me], sibling, view)

    def from_line(h, d):
        s = slot(ahead(na - d), b, core)
        arrived(gbuf.at[h, s], g_r.at[h, s])
        for e in range(1, nb):
            push(gbuf.at[h, s], gbuf.at[h, s], gb_s.at[h, d, e - 1], g_r.at[h, s],
                 slot(a, beside(e), core), view)
        push(gbuf.at[h, s], gbuf.at[h, s], gc_s.at[h, d, 0], g_r.at[h, s], sibling, view)

    def from_across(h):
        for d in range(na):
            for e in range(1, nb):
                s = slot(ahead(na - d), beside(nb - e), core)
                arrived(gbuf.at[h, s], g_r.at[h, s])
                push(gbuf.at[h, s], gbuf.at[h, s], gc_s.at[h, d, e], g_r.at[h, s], sibling, view)

    for h in range(CHUNKS):
        gbuf[h, me] = gl[h]
    bdw[...] = jnp.zeros_like(bdw)
    rbuf[...] = jnp.zeros_like(rbuf)
    for j in range(GROUP):
        bdw[j * RL:(j + 1) * RL, j * LIGHTS:j * LIGHTS + L] = lightt_ref[...]
    vcol[...] = jnp.zeros_like(vcol)
    vrow[...] = jnp.zeros_like(vrow)
    vcol[:views, :] = vt_ref[...].T
    vrow[:, :views] = vt_ref[...]
    weights[...] = jnp.broadcast_to(mask_ref[...].astype(F32), (LIGHTS, views)).T
    meas_copy.wait()
    mwide[...] = meas[...].astype(F32)
    turns = -(-texels // (CHUNKS * (na - 1)))
    t = 0
    for h in range(CHUNKS):
        for d in range(1, na):
            from_line(h, d)
            for _ in range(turns):
                if t < texels:
                    mturn[t] = mwide[:, t, :].T
                    t += 1

    u_bf = u_ref[...].astype(BF)

    def stacked(h):
        if rows % 16 == 0:
            return gbuf[h].reshape(tex_count * rows, part * RL)
        return jnp.concatenate(
            [gbuf[h, j].astype(F32) for j in range(tex_count)], axis=0).astype(BF)

    for h in range(CHUNKS):
        from_across(h)
        for ai in range(na):
            for bi in range(nb):
                s = slot(ai, bi, 1 - core)
                arrived(gbuf.at[h, s], g_r.at[h, s])
        proj = jnp.dot(u_bf, stacked(h), preferred_element_type=F32)
        for j in range(part):
            p3[h, j] = proj[:, j * RL:(j + 1) * RL]
        for t in range(0, texels, 2):
            pair = jnp.concatenate([p3[h, :, t, :], p3[h, :, t + 1, :]], axis=1)
            pall[h, view, :, t * RL:(t + 2) * RL] = pair.astype(BF)
        for w in range(1, view_count):
            push(pall.at[h, view], pall.at[h, view], p_s.at[h, w - 1], p_r.at[h, view],
                 me, other(w))
    v_bf = vcol[...].astype(BF)
    vt_bf = vrow[...].astype(BF)
    for h in range(CHUNKS):
        for w in range(1, view_count):
            arrived(pall.at[h, other(w)], p_r.at[h, other(w)])

    def lanes(k):
        return slice(k * GROUP * RL, (k + 1) * GROUP * RL)

    def p_group(k):
        pieces = [pall[h, w, :, lanes(k)] for w in range(view_count) for h in range(CHUNKS)]
        if part % 16 == 0:
            return jnp.concatenate(pieces, axis=0)
        return jnp.concatenate([piece.astype(F32) for piece in pieces], axis=0).astype(BF)

    for k in range(groups):
        qbuf[k] = jnp.dot(v_bf, p_group(k), preferred_element_type=F32).astype(BF)
    q_all = qbuf[...].reshape(groups * padded, GROUP * RL)
    mask = weights[:, :L]
    for j in range(GROUP):
        cols = slice(j * LIGHTS, (j + 1) * LIGHTS)
        approx = jnp.dot(q_all, bdw[:, cols], preferred_element_type=F32)
        for k in range(groups):
            piece = approx[k * padded:k * padded + views, :L]
            resid = mask * (SCALING * piece - mturn[k * GROUP + j])
            rbuf[k, :views, j * LIGHTS:j * LIGHTS + L] = resid.astype(BF)
    r_all = rbuf[...].reshape(groups * padded, GROUP * LIGHTS)
    s_all = lax.dot_general(r_all, bdw[...], NT, preferred_element_type=F32).astype(BF)
    for k in range(groups):
        s4 = s_all[k * padded:(k + 1) * padded]
        y4 = jnp.dot(vt_bf, s4, preferred_element_type=F32).astype(BF)
        for w in range(view_count):
            for h in range(CHUNKS):
                first = w * band + h * part
                ysend[h, w, :, lanes(k)] = y4[first:first + part]
    for h in range(CHUNKS):
        for w in range(1, view_count):
            push(ysend.at[h, other(w)], yrecv.at[h, w - 1], y_s.at[h, w - 1], y_r.at[h, w - 1],
                 me, other(w))
    gv = jnp.zeros((RV, padded), F32)
    for k in range(groups):
        s4 = s_all[k * padded:(k + 1) * padded]
        gv = gv + lax.dot_general(p_group(k), s4, NT, preferred_element_type=F32)

    def gv_start(i, value):
        gvs[i] = value
        partner = me + (1 << i) - 2 * (1 << i) * lax.rem(me // (1 << i), 2)
        push(gvs.at[i], gvr.at[i], gv_s.at[i], gv_r.at[i], partner, view)

    def gv_next(i):
        arrived(gvr.at[i], gv_r.at[i])
        value = gvs[i] + gvr[i]
        if i + 1 < steps:
            gv_start(i + 1, value)
        else:
            vt_out[...] = vt_ref[...] - rate_view * value[:, :views]

    gv_start(0, SCALING * gv)

    order = [d % na for d in range(1, na + 1)]
    y_bf = []
    for h in range(CHUNKS):
        total = ysend[h, view].astype(F32)
        for w in range(1, view_count):
            arrived(yrecv.at[h, w - 1], y_r.at[h, w - 1])
            total = total + yrecv[h, w - 1].astype(F32)
        for t in range(texels):
            ysum[h, :, t, :] = total[:, t * RL:(t + 1) * RL]
        for j in range(0, part, 2):
            pair = jnp.concatenate([ysum[h, j], ysum[h, j + 1]], axis=1)
            yflat[h, :, j * RL:(j + 2) * RL] = pair.astype(BF)
        y_bf.append(yflat[h])
        grad = SCALING * lax.dot_general(u_bf, y_bf[h], TN, preferred_element_type=F32)
        for j in range(tex_count):
            rs[h, j] = grad[j * rows:(j + 1) * rows].astype(BF)
        for e in list(range(1, nb)) + [0]:
            for d in order:
                push(rs.at[h, slot(ahead(d), beside(e), 1 - core)], rc.at[h, d, e],
                     c_s.at[h, d, e], c_r.at[h, d, e], sibling, view)

    partial = jnp.zeros((texels, RT), F32)
    for h in range(CHUNKS):
        partial = partial + lax.dot_general(y_bf[h], stacked(h), NT, preferred_element_type=F32)
    us[...] = SCALING * partial
    for w in range(1, view_count):
        push(us, ur.at[w - 1], u_s.at[w - 1], u_r.at[w - 1], me, other(w))
    gv_next(0)

    for h in range(CHUNKS):
        for e in range(1, nb):
            for d in order:
                s = slot(ahead(d), beside(e), core)
                arrived(rc.at[h, d, e], c_r.at[h, d, e])
                rs[h, s] = (rs[h, s].astype(F32) + rc[h, d, e].astype(F32)).astype(BF)
                push(rs.at[h, s], xr.at[h, d, e - 1], x_s.at[h, d, e - 1], x_r.at[h, d, e - 1],
                     slot(a, beside(e), core), view)
        if h + 1 < steps:
            gv_next(h + 1)
    own = []
    for h in range(CHUNKS):
        for d in order:
            s = slot(ahead(d), b, core)
            arrived(rc.at[h, d, 0], c_r.at[h, d, 0])
            block = rs[h, s].astype(F32) + rc[h, d, 0].astype(F32)
            for e in range(1, nb):
                arrived(xr.at[h, d, e - 1], x_r.at[h, d, e - 1])
                block = block + xr[h, d, e - 1].astype(F32)
            if d:
                rs[h, s] = block.astype(BF)
                push(rs.at[h, s], zr.at[h, d - 1], z_s.at[h, d - 1], z_r.at[h, d - 1],
                     slot(ahead(d), b, core), view)
        own.append(block)
    for i in range(CHUNKS + 1, steps):
        gv_next(i)
    total_u = us[...]
    for w in range(1, view_count):
        arrived(ur.at[w - 1], u_r.at[w - 1])
        total_u = total_u + ur[w - 1]
    u_out[...] = u_ref[...] - rate_tex * total_u
    for h in range(CHUNKS):
        block = own[h]
        for d in range(1, na):
            arrived(zr.at[h, d - 1], z_r.at[h, d - 1])
            block = block + zr[h, d - 1].astype(F32)
        block = rate_core * block
        for j in range(part):
            i = h * part + j
            core_out[:, i, :] = core_ref[:, i, :] - block[:, j * RL:(j + 1) * RL]
    for copy in pending:
        copy.wait_send()


def per_device(measured, view_mask, tex_factor, view_factor, light_factor, core_tensor):
    tex_count = lax.axis_size("tex")
    view_count = lax.axis_size("view")
    texels, views, _ = measured.shape
    rows, band, _ = core_tensor.shape
    part = band // CHUNKS
    cut = part * RL
    texels_all = texels * tex_count
    nb = tex_count // (2 * LINE)
    steps = tex_count.bit_length() - 1
    peers = max(view_count - 1, 1)
    across = max(nb - 1, 1)
    padded = 16 * (-(-views // 16))
    groups = texels // GROUP
    rates = (
        RT / (VALID * L),
        RV / (texels_all * L),
        RT * RV * RL / (texels_all * VALID * L),
    )
    vmem = pl.BlockSpec(memory_space=pltpu.VMEM)
    dma = pltpu.SemaphoreType.DMA
    tex_new, view_new, core_new = pl.pallas_call(
        functools.partial(kernel, tex_count, view_count, rates),
        out_shape=(
            jax.ShapeDtypeStruct((texels, RT), F32),
            jax.ShapeDtypeStruct((RV, views), F32),
            jax.ShapeDtypeStruct((rows, band, RL), F32),
        ),
        in_specs=[vmem] * 5 + [pl.BlockSpec(memory_space=pl.ANY)],
        out_specs=(vmem, vmem, vmem),
        scratch_shapes=[
            pltpu.VMEM((CHUNKS, rows, cut), BF),
            pltpu.VMEM((CHUNKS, tex_count, rows, cut), BF),
            pltpu.VMEM((L, texels, views), BF),
            pltpu.VMEM((L, texels, views), F32),
            pltpu.VMEM((texels, views, L), F32),
            pltpu.VMEM((views, LIGHTS), F32),
            pltpu.VMEM((padded, RV), F32),
            pltpu.VMEM((RV, padded), F32),
            pltpu.VMEM((GROUP * RL, GROUP * LIGHTS), BF),
            pltpu.VMEM((groups, padded, GROUP * RL), BF),
            pltpu.VMEM((groups, padded, GROUP * LIGHTS), BF),
            pltpu.VMEM((CHUNKS, part, texels, RL), F32),
            pltpu.VMEM((CHUNKS, view_count, part, texels * RL), BF),
            pltpu.VMEM((CHUNKS, view_count, part, texels * RL), BF),
            pltpu.VMEM((CHUNKS, peers, part, texels * RL), BF),
            pltpu.VMEM((CHUNKS, part, texels, RL), F32),
            pltpu.VMEM((CHUNKS, texels, cut), BF),
            pltpu.VMEM((texels, RT), F32),
            pltpu.VMEM((peers, texels, RT), F32),
            pltpu.VMEM((steps, RV, padded), F32),
            pltpu.VMEM((steps, RV, padded), F32),
            pltpu.VMEM((CHUNKS, tex_count, rows, cut), BF),
            pltpu.VMEM((CHUNKS, LINE, nb, rows, cut), BF),
            pltpu.VMEM((CHUNKS, LINE, across, rows, cut), BF),
            pltpu.VMEM((CHUNKS, LINE - 1, rows, cut), BF),
            dma, dma((CHUNKS, LINE - 1)), dma((CHUNKS, LINE, across)), dma((CHUNKS, LINE, nb)),
            dma((CHUNKS, tex_count)),
            dma((CHUNKS, peers)), dma((CHUNKS, view_count)),
            dma((CHUNKS, peers)), dma((CHUNKS, peers)),
            dma((peers,)), dma((peers,)), dma((steps,)), dma((steps,)),
            dma((CHUNKS, LINE, nb)), dma((CHUNKS, LINE, nb)),
            dma((CHUNKS, LINE, across)), dma((CHUNKS, LINE, across)),
            dma((CHUNKS, LINE - 1)), dma((CHUNKS, LINE - 1)),
        ],
        compiler_params=pltpu.CompilerParams(
            collective_id=0, has_side_effects=True, vmem_limit_bytes=48 * 1024 * 1024),
        cost_estimate=pl.CostEstimate(flops=10**9, bytes_accessed=10**7, transcendentals=0),
    )(core_tensor, tex_factor, view_factor.T, view_mask.reshape(1, views), light_factor.T,
      jnp.transpose(measured, (2, 0, 1)))
    return tex_new, view_new.T, core_new


def solution(mesh):
    return jax.shard_map(
        per_device,
        mesh=mesh,
        in_specs=(
            P("tex", "view", None),
            P("view"),
            P("tex", None),
            P("view", None),
            P(),
            P("tex", "view", None),
        ),
        out_specs=(P("tex", None), P("view", None), P("tex", "view", None)),
        check_vma=False,
    )
```

time: 176 us -> 48.6 us (0.28)
  blocking collectives: 76 us -> 0 us
  waiting for transfers between devices: 63.3 us -> 0 us
  Pallas kernels: 0 us -> 40.6 us
  between operations: 13.9 us -> 0.65 us
  local copies, waits for them, and re-layouts: 14 us -> 6.96 us
  matrix products: 5.36 us -> 0 us
  other arithmetic: 2.73 us -> 0 us
    psum x2 -> x0, blocking collectives: 68.9 us -> none  [the longest x1 61.3 us: per_device(): grad_view = lax.psum(view_part, 'tex')]
    all_gather x1 -> x0, waiting for transfers between devices: 51.5 us -> none  [per_device(): core_whole = lax.all_gather(core_band, 'tex', axis=0, tiled=True)]
    pallas_call x0 -> x1, Pallas kernels: none -> 40.6 us  [per_device(): pl.pallas_call(functools.partial(kernel, tex_count, view_count, rates), o...]
    reduce_scatter x1 -> x0, waiting for transfers between devices: 11.7 us -> none  [per_device(): lax.psum_scatter(partial_y.astype(jnp.bfloat16), 'view', scatter_dimensio...]
    all_gather x1 -> x0, blocking collectives: 7.12 us -> none  [per_device(): core_band = lax.all_gather(core_bf, 'view', axis=1, tiled=True)]
    all_gather x2 -> x0, local copies, waits for them, and re-layouts: 5.7 us -> none  [the longest x1 4.92 us: per_device(): core_whole = lax.all_gather(core_band, 'tex', axis=0, tiled=True)]
    dot_general x7 -> x0, matrix products: 5.36 us -> none  [the longest x1 1.82 us: per_device(): jnp.einsum('tvl,lc->tvc', resid, light_factor, preferred_element_type=jnp...]
    sub x3 -> x0, other arithmetic: 1.98 us -> none  [the longest x1 0.74 us: per_device(): core_now = core_now - rate_core * grad_core.reshape(core_now.shape)]
  transfers between devices with their start and end apart: 3 -> 0, of which waited for: 2 -> 0; matrix products, arithmetic and copies ran while one was open for 1% -> 0% of each run, Pallas kernels for 0% -> 0%
where the time goes in v2:
time: 48.6 us; the launch traced here: 48.2 us
  Pallas kernels  40.6 us (84%)
  local copies, waits for them, and re-layouts  6.96 us (14%)
  between operations  0.65 us (1%)
    pallas_call x1, Pallas kernels, per_device(): pl.pallas_call(functools.partial(kernel, tex_count, view_count, rates), o...  40.6 us
    unnamed x15, local copies, waits for them, and re-layouts  6.96 us

profile of v2, /device:TPU:0, one launch (start us, length us, event | category | flops | bytes accessed | tf_op | source)
XLA Modules:
  0.0 48.2 jit_solution(3747763221036742210)
XLA Ops:
  0.6 0.0 copy-start.5
  0.6 0.6 %copy-done.5 = s32[80]{0:T(128)S(1)} copy-done((s32[80]{0:T(128)S(1)}, s32[80]{0:T(128)}, u32[]{:S(2)}) %copy-start.5) | copy-done | bytes 344
  1.3 0.0 copy-start
  1.3 1.2 %copy-done = bf16[24,80,151]{1,0,2:T(8,128)(2,1)S(1)} copy-done((bf16[24,80,151]{1,0,2:T(8,128)(2,1)S(1)}, bf16[24,80,151]{1,0,2:T(8,128)(2,1)}, u32[]{:S(2)}) %copy-start) | copy-done | bytes 579864
  2.5 0.0 copy-start.1
  2.5 0.9 %copy-done.1 = f32[16,32,64]{2,1,0:T(8,128)S(1)} copy-done((f32[16,32,64]{2,1,0:T(8,128)S(1)}, f32[16,32,64]{2,1,0:T(8,128)}, u32[]{:S(2)}) %copy-start.1) | copy-done | bytes 131096
  3.4 0.0 copy-start.2
  3.4 0.8 %copy-done.2 = f32[80,64]{0,1:T(8,128)S(1)} copy-done((f32[80,64]{0,1:T(8,128)S(1)}, f32[80,64]{0,1:T(8,128)}, u32[]{:S(2)}) %copy-start.2) | copy-done | bytes 20504
  4.2 0.0 copy-start.3
  4.2 0.8 %copy-done.3 = bf16[151,64]{0,1:T(8,128)(2,1)S(1)} copy-done((bf16[151,64]{0,1:T(8,128)(2,1)S(1)}, bf16[151,64]{0,1:T(8,128)(2,1)}, u32[]{:S(2)}) %copy-start.3) | copy-done | bytes 19352
  4.9 0.0 copy-start.4
  4.9 0.7 %copy-done.4 = f32[24,256]{1,0:T(8,128)S(1)} copy-done((f32[24,256]{1,0:T(8,128)S(1)}, f32[24,256]{1,0:T(8,128)}, u32[]{:S(2)}) %copy-start.4) | copy-done | bytes 24600
  5.7 40.6 %shard_map.85 = (f32[24,256]{1,0:T(8,128)S(1)}, f32[64,80]{1,0:T(8,128)S(1)}, f32[16,32,64]{2,1,0:T(8,128)S(1)}) custom-call(f32[16,32,64]{2,1,0:T(8,128)S(1)} %copy-done.1, f32[24,256]{1,0:T(8,128)S(1)} %copy-done.4, f32[64,80]{1,0:T(8,128)S(1)} %bitcast.7, s32[1,80]{1,0:T(1,128)S(1)} %bitcast.9, bf16[64,151]{1,0:T(8,128)(2,1)S(1)} %bitcast.8, ...), custom_call_target="tpu_custom_call" | custom-call | flops 1000000000 | bytes 10000000 | tf_op jit(solution)/shard_map/pallas_call | solution.py:316
  46.3 0.6 %copy.12 = f32[24,256]{1,0:T(8,128)} copy(f32[24,256]{1,0:T(8,128)S(1)} %get-tuple-element.12) | data formatting | bytes 49152
  46.9 0.6 %copy.13 = f32[80,64]{0,1:T(8,128)} copy(f32[80,64]{0,1:T(8,128)S(1)} %bitcast.5) | data formatting | bytes 40960
  47.5 0.7 %copy.14 = f32[16,32,64]{2,1,0:T(8,128)} copy(f32[16,32,64]{2,1,0:T(8,128)S(1)} %get-tuple-element.14) | data formatting | bytes 262144
Async XLA Ops:
  0.6 0.7 %copy-start.5 = (s32[80]{0:T(128)S(1)}, s32[80]{0:T(128)}, u32[]{:S(2)}) copy-start(s32[80]{0:T(128)} %param.7) | copy-start | bytes 964
  1.3 1.2 %copy-start = (bf16[24,80,151]{1,0,2:T(8,128)(2,1)S(1)}, bf16[24,80,151]{1,0,2:T(8,128)(2,1)}, u32[]{:S(2)}) copy-start(bf16[24,80,151]{1,0,2:T(8,128)(2,1)} %param.6) | copy-start | bytes 1739524
  2.5 0.9 %copy-start.1 = (f32[16,32,64]{2,1,0:T(8,128)S(1)}, f32[16,32,64]{2,1,0:T(8,128)}, u32[]{:S(2)}) copy-start(f32[16,32,64]{2,1,0:T(8,128)} %core_ref.1) | copy-start | bytes 393220
  3.4 0.8 %copy-start.2 = (f32[80,64]{0,1:T(8,128)S(1)}, f32[80,64]{0,1:T(8,128)}, u32[]{:S(2)}) copy-start(f32[80,64]{0,1:T(8,128)} %param.9) | copy-start | bytes 61444
  4.2 0.8 %copy-start.3 = (bf16[151,64]{0,1:T(8,128)(2,1)S(1)}, bf16[151,64]{0,1:T(8,128)(2,1)}, u32[]{:S(2)}) copy-start(bf16[151,64]{0,1:T(8,128)(2,1)} %param.10) | copy-start | bytes 57988
  4.9 0.7 %copy-start.4 = (f32[24,256]{1,0:T(8,128)S(1)}, f32[24,256]{1,0:T(8,128)}, u32[]{:S(2)}) copy-start(f32[24,256]{1,0:T(8,128)} %u_ref.1) | copy-start | bytes 73732

commit v3 on v2

--- a/solution.py
+++ b/solution.py
@@ -26,12 +26,13 @@
 
 def kernel(
     tex_count, view_count, rates,
-    core_ref, u_ref, vt_ref, mask_ref, lightt_ref, meas_hbm,
+    core_hbm, u_hbm, vt_hbm, mask_hbm, lightt_hbm, meas_hbm,
     u_out, vt_out, core_out,
+    core_ref, u_ref, vt_ref, mask_ref, lightt_ref, usib, uturn,
     gl, gbuf, meas, mwide, mturn, weights, vcol, vrow, bdw, qbuf, rbuf, p3, pall,
-    ysend, yrecv, ysum, yflat, us, ur, gvs, gvr, rs, rc, xr, zr,
-    meas_sem, ga_s, gb_s, gc_s, g_r, p_s, p_r, y_s, y_r, u_s, u_r, gv_s, gv_r,
-    c_s, c_r, x_s, x_r, z_s, z_r,
+    ysend, yrecv, ysum, yflat, ytot, ysib, us, ur, gvs, gvr, xs, xr, held, zs, zr,
+    in_sem, w_s, w_r, ga_s, gb_s, gc_s, g_r, p_s, p_r, y_s, y_r, u_s, u_r, gv_s, gv_r,
+    h_s, h_r, x_s, x_r, z_s, z_r,
 ):
     na = LINE
     nb = tex_count // (2 * na)
@@ -82,8 +83,14 @@
     peers += [(me, other(w)) for w in range(1, view_count)]
     for peer in peers:
         pl.semaphore_signal(barrier, inc=1, device_id=peer, device_id_type=MESH)
-    meas_copy = pltpu.make_async_copy(meas_hbm, meas, meas_sem)
-    meas_copy.start()
+    fetches = [
+        pltpu.make_async_copy(src, dst, in_sem.at[i]) for i, (src, dst) in enumerate((
+            (core_hbm, core_ref), (u_hbm, u_ref), (meas_hbm, meas),
+            (vt_hbm, vt_ref), (mask_hbm, mask_ref), (lightt_hbm, lightt_ref)))
+    ]
+    for fetch in fetches:
+        fetch.start()
+    fetches[0].wait()
     for i in range(0, band, 2):
         pair = jnp.concatenate([core_ref[:, i, :], core_ref[:, i + 1, :]], axis=1).astype(BF)
         h, o = divmod(i, part)
@@ -98,6 +105,8 @@
             push(gl.at[h], gbuf.at[h, me], ga_s.at[h, d - 1], g_r.at[h, me],
                  slot(ahead(d), b, core), view)
         push(gl.at[h], gbuf.at[h, me], gc_s.at[h, 0, 0], g_r.at[h, me], sibling, view)
+    fetches[1].wait()
+    push(u_ref, usib, w_s, w_r, sibling, view)
 
     def from_line(h, d):
         s = slot(ahead(na - d), b, core)
@@ -118,6 +127,8 @@
         gbuf[h, me] = gl[h]
     bdw[...] = jnp.zeros_like(bdw)
     rbuf[...] = jnp.zeros_like(rbuf)
+    for fetch in fetches[2:]:
+        fetch.wait()
     for j in range(GROUP):
         bdw[j * RL:(j + 1) * RL, j * LIGHTS:j * LIGHTS + L] = lightt_ref[...]
     vcol[...] = jnp.zeros_like(vcol)
@@ -125,7 +136,6 @@
     vcol[:views, :] = vt_ref[...].T
     vrow[:, :views] = vt_ref[...]
     weights[...] = jnp.broadcast_to(mask_ref[...].astype(F32), (LIGHTS, views)).T
-    meas_copy.wait()
     mwide[...] = meas[...].astype(F32)
     turns = -(-texels // (CHUNKS * (na - 1)))
     t = 0
@@ -138,6 +148,10 @@
                     t += 1
 
     u_bf = u_ref[...].astype(BF)
+    arrived(usib, w_r)
+    turned = jnp.concatenate([u_ref[...], usib[...]], axis=0).T
+    for j in range(tex_count):
+        uturn[j] = turned[j * rows:(j + 1) * rows]
 
     def stacked(h):
         if rows % 16 == 0:
@@ -220,58 +234,64 @@
     gv_start(0, SCALING * gv)
 
     order = [d % na for d in range(1, na + 1)]
-    y_bf = []
+
+    def turn(h, first, values):
+        for t in range(texels):
+            ysum[h, :, first + t, :] = values[:, t * RL:(t + 1) * RL]
+
     for h in range(CHUNKS):
         total = ysend[h, view].astype(F32)
         for w in range(1, view_count):
             arrived(yrecv.at[h, w - 1], y_r.at[h, w - 1])
             total = total + yrecv[h, w - 1].astype(F32)
-        for t in range(texels):
-            ysum[h, :, t, :] = total[:, t * RL:(t + 1) * RL]
+        ytot[h] = total.astype(BF)
+        push(ytot.at[h], ysib.at[h], h_s.at[h], h_r.at[h], sibling, view)
+        turn(h, 0, total)
+
+    def u_rows(e):
+        return jnp.concatenate(
+            [uturn[slot(ahead(d), beside(e), core)] for d in order], axis=0).astype(BF)
+
+    u_parts = [u_rows(e) for e in range(nb)]
+    for h in range(CHUNKS):
+        arrived(ysib.at[h], h_r.at[h])
+        turn(h, texels, ysib[h].astype(F32))
         for j in range(0, part, 2):
             pair = jnp.concatenate([ysum[h, j], ysum[h, j + 1]], axis=1)
             yflat[h, :, j * RL:(j + 2) * RL] = pair.astype(BF)
-        y_bf.append(yflat[h])
-        grad = SCALING * lax.dot_general(u_bf, y_bf[h], TN, preferred_element_type=F32)
-        for j in range(tex_count):
-            rs[h, j] = grad[j * rows:(j + 1) * rows].astype(BF)
-        for e in list(range(1, nb)) + [0]:
-            for d in order:
-                push(rs.at[h, slot(ahead(d), beside(e), 1 - core)], rc.at[h, d, e],
-                     c_s.at[h, d, e], c_r.at[h, d, e], sibling, view)
-
-    partial = jnp.zeros((texels, RT), F32)
-    for h in range(CHUNKS):
-        partial = partial + lax.dot_general(y_bf[h], stacked(h), NT, preferred_element_type=F32)
-    us[...] = SCALING * partial
+        for e in range(1, nb):
+            grad = SCALING * jnp.dot(u_parts[e], yflat[h], preferred_element_type=F32)
+            for i, d in enumerate(order):
+                xs[h, d, e - 1] = grad[i * rows:(i + 1) * rows].astype(BF)
+                push(xs.at[h, d, e - 1], xr.at[h, d, e - 1], x_s.at[h, d, e - 1],
+                     x_r.at[h, d, e - 1], slot(a, beside(e), core), view)
+        grad = SCALING * jnp.dot(u_parts[0], yflat[h], preferred_element_type=F32)
+        for i, d in enumerate(order):
+            held[h, d] = grad[i * rows:(i + 1) * rows]
+        if h == 0:
+            gv_next(0)
+
+    partial = jnp.zeros((2 * texels, RT), F32)
+    for h in range(CHUNKS):
+        partial = partial + lax.dot_general(yflat[h], stacked(h), NT, preferred_element_type=F32)
+    us[...] = SCALING * partial[:texels]
     for w in range(1, view_count):
         push(us, ur.at[w - 1], u_s.at[w - 1], u_r.at[w - 1], me, other(w))
-    gv_next(0)
-
-    for h in range(CHUNKS):
-        for e in range(1, nb):
-            for d in order:
-                s = slot(ahead(d), beside(e), core)
-                arrived(rc.at[h, d, e], c_r.at[h, d, e])
-                rs[h, s] = (rs[h, s].astype(F32) + rc[h, d, e].astype(F32)).astype(BF)
-                push(rs.at[h, s], xr.at[h, d, e - 1], x_s.at[h, d, e - 1], x_r.at[h, d, e - 1],
-                     slot(a, beside(e), core), view)
-        if h + 1 < steps:
-            gv_next(h + 1)
+
     own = []
     for h in range(CHUNKS):
         for d in order:
-            s = slot(ahead(d), b, core)
-            arrived(rc.at[h, d, 0], c_r.at[h, d, 0])
-            block = rs[h, s].astype(F32) + rc[h, d, 0].astype(F32)
+            block = held[h, d]
             for e in range(1, nb):
                 arrived(xr.at[h, d, e - 1], x_r.at[h, d, e - 1])
                 block = block + xr[h, d, e - 1].astype(F32)
             if d:
-                rs[h, s] = block.astype(BF)
-                push(rs.at[h, s], zr.at[h, d - 1], z_s.at[h, d - 1], z_r.at[h, d - 1],
+                zs[h, d - 1] = block.astype(BF)
+                push(zs.at[h, d - 1], zr.at[h, d - 1], z_s.at[h, d - 1], z_r.at[h, d - 1],
                      slot(ahead(d), b, core), view)
         own.append(block)
+        if h + 1 < steps:
+            gv_next(h + 1)
     for i in range(CHUNKS + 1, steps):
         gv_next(i)
     total_u = us[...]
@@ -290,6 +310,17 @@
             core_out[:, i, :] = core_ref[:, i, :] - block[:, j * RL:(j + 1) * RL]
     for copy in pending:
         copy.wait_send()
+
+
+def write_out(a_ref, b_ref, c_ref, a_out, b_out, c_out, sems):
+    copies = [
+        pltpu.make_async_copy(src, dst, sems.at[i])
+        for i, (src, dst) in enumerate(((c_ref, c_out), (a_ref, a_out), (b_ref, b_out)))
+    ]
+    for copy in copies:
+        copy.start()
+    for copy in copies:
+        copy.wait()
 
 
 def per_device(measured, view_mask, tex_factor, view_factor, light_factor, core_tensor):
@@ -312,6 +343,7 @@
         RT * RV * RL / (texels_all * VALID * L),
     )
     vmem = pl.BlockSpec(memory_space=pltpu.VMEM)
+    hbm = pl.BlockSpec(memory_space=pltpu.HBM)
     dma = pltpu.SemaphoreType.DMA
     tex_new, view_new, core_new = pl.pallas_call(
         functools.partial(kernel, tex_count, view_count, rates),
@@ -320,9 +352,16 @@
             jax.ShapeDtypeStruct((RV, views), F32),
             jax.ShapeDtypeStruct((rows, band, RL), F32),
         ),
-        in_specs=[vmem] * 5 + [pl.BlockSpec(memory_space=pl.ANY)],
+        in_specs=[hbm] * 6,
         out_specs=(vmem, vmem, vmem),
         scratch_shapes=[
+            pltpu.VMEM((rows, band, RL), F32),
+            pltpu.VMEM((texels, RT), F32),
+            pltpu.VMEM((RV, views), F32),
+            pltpu.VMEM((1, views), jnp.int32),
+            pltpu.VMEM((RL, L), BF),
+            pltpu.VMEM((texels, RT), F32),
+            pltpu.VMEM((tex_count, rows, 2 * texels), F32),
             pltpu.VMEM((CHUNKS, rows, cut), BF),
             pltpu.VMEM((CHUNKS, tex_count, rows, cut), BF),
             pltpu.VMEM((L, texels, views), BF),
@@ -338,30 +377,45 @@
             pltpu.VMEM((CHUNKS, view_count, part, texels * RL), BF),
             pltpu.VMEM((CHUNKS, view_count, part, texels * RL), BF),
             pltpu.VMEM((CHUNKS, peers, part, texels * RL), BF),
-            pltpu.VMEM((CHUNKS, part, texels, RL), F32),
-            pltpu.VMEM((CHUNKS, texels, cut), BF),
+            pltpu.VMEM((CHUNKS, part, 2 * texels, RL), F32),
+            pltpu.VMEM((CHUNKS, 2 * texels, cut), BF),
+            pltpu.VMEM((CHUNKS, part, texels * RL), BF),
+            pltpu.VMEM((CHUNKS, part, texels * RL), BF),
             pltpu.VMEM((texels, RT), F32),
             pltpu.VMEM((peers, texels, RT), F32),
             pltpu.VMEM((steps, RV, padded), F32),
             pltpu.VMEM((steps, RV, padded), F32),
-            pltpu.VMEM((CHUNKS, tex_count, rows, cut), BF),
-            pltpu.VMEM((CHUNKS, LINE, nb, rows, cut), BF),
             pltpu.VMEM((CHUNKS, LINE, across, rows, cut), BF),
+            pltpu.VMEM((CHUNKS, LINE, across, rows, cut), BF),
+            pltpu.VMEM((CHUNKS, LINE, rows, cut), F32),
             pltpu.VMEM((CHUNKS, LINE - 1, rows, cut), BF),
-            dma, dma((CHUNKS, LINE - 1)), dma((CHUNKS, LINE, across)), dma((CHUNKS, LINE, nb)),
+            pltpu.VMEM((CHUNKS, LINE - 1, rows, cut), BF),
+            dma((6,)), dma, dma, dma((CHUNKS, LINE - 1)), dma((CHUNKS, LINE, across)), dma((CHUNKS, LINE, nb)),
             dma((CHUNKS, tex_count)),
             dma((CHUNKS, peers)), dma((CHUNKS, view_count)),
             dma((CHUNKS, peers)), dma((CHUNKS, peers)),
             dma((peers,)), dma((peers,)), dma((steps,)), dma((steps,)),
-            dma((CHUNKS, LINE, nb)), dma((CHUNKS, LINE, nb)),
+            dma((CHUNKS,)), dma((CHUNKS,)),
             dma((CHUNKS, LINE, across)), dma((CHUNKS, LINE, across)),
             dma((CHUNKS, LINE - 1)), dma((CHUNKS, LINE - 1)),
         ],
         compiler_params=pltpu.CompilerParams(
             collective_id=0, has_side_effects=True, vmem_limit_bytes=48 * 1024 * 1024),
         cost_estimate=pl.CostEstimate(flops=10**9, bytes_accessed=10**7, transcendentals=0),
-    )(core_tensor, tex_factor, view_factor.T, view_mask.reshape(1, views), light_factor.T,
-      jnp.transpose(measured, (2, 0, 1)))
+    )(*(pltpu.with_memory_space_constraint(x, pltpu.HBM) for x in (
+        core_tensor, tex_factor, view_factor.T, view_mask.reshape(1, views), light_factor.T,
+        jnp.transpose(measured, (2, 0, 1)))))
+    tex_new, view_new, core_new = pl.pallas_call(
+        write_out,
+        out_shape=(
+            jax.ShapeDtypeStruct((texels, RT), F32),
+            jax.ShapeDtypeStruct((RV, views), F32),
+            jax.ShapeDtypeStruct((rows, band, RL), F32),
+        ),
+        in_specs=[vmem] * 3,
+        out_specs=(hbm, hbm, hbm),
+        scratch_shapes=[dma((3,))],
+    )(tex_new, view_new, core_new)
     return tex_new, view_new.T, core_new
 
 

time: 48.6 us -> 44.8 us (0.922)
  local copies, waits for them, and re-layouts: 6.96 us -> 1.9 us
  Pallas kernels: 40.6 us -> 42.1 us
    unnamed x15 -> x6, local copies, waits for them, and re-layouts: 6.96 us -> 1.9 us
    pallas_call x0 -> x1, Pallas kernels: none -> 1.72 us  [per_device(): pl.pallas_call(write_out, out_shape=(jax.ShapeDtypeStruct((texels, RT), F...]
where the time goes in v3:
time: 44.8 us; the launch traced here: 44.6 us
  Pallas kernels  42.1 us (94%)
  local copies, waits for them, and re-layouts  1.9 us (4%)
  between operations  0.65 us (1%)
    pallas_call x1, Pallas kernels, per_device(): pl.pallas_call(functools.partial(kernel, tex_count, view_count, rates), o...  40.4 us
    unnamed x6, local copies, waits for them, and re-layouts  1.9 us
    pallas_call x1, Pallas kernels, per_device(): pl.pallas_call(write_out, out_shape=(jax.ShapeDtypeStruct((texels, RT), F...  1.72 us

profile of v3, /device:TPU:0, one launch (start us, length us, event | category | flops | bytes accessed | tf_op | source)
XLA Modules:
  0.0 44.6 jit_solution(3104172594692905238)
XLA Ops:
  0.6 40.4 %shard_map.85 = (f32[24,256]{1,0:T(8,128)S(1)}, f32[64,80]{1,0:T(8,128)S(1)}, f32[16,32,64]{2,1,0:T(8,128)S(1)}) custom-call(f32[16,32,64]{2,1,0:T(8,128)} %core_hbm.1, f32[24,256]{1,0:T(8,128)} %u_hbm.1, f32[64,80]{1,0:T(8,128)} %bitcast.6, s32[1,80]{1,0:T(1,128)} %bitcast.9, bf16[64,151]{1,0:T(8,128)(2,1)} %bitcast.7, bf16[151,24,80]{2,1,0:T(8,128)(2,1)} %bitcast.5), custom_call_target="tpu_custom_call" | custom-call | flops 1000000000 | bytes 10000000 | tf_op jit(solution)/shard_map/pallas_call | solution.py:348
  41.0 0.0 copy-start
  41.0 0.7 %copy-done = f32[16,32,64]{2,1,0:T(8,128)} copy-done((f32[16,32,64]{2,1,0:T(8,128)}, f32[16,32,64]{2,1,0:T(8,128)S(1)}, u32[]{:S(2)}) %copy-start) | copy-done | bytes 131096
  41.7 0.0 copy-start.1
  41.7 0.6 %copy-done.1 = f32[64,80]{1,0:T(8,128)} copy-done((f32[64,80]{1,0:T(8,128)}, f32[64,80]{1,0:T(8,128)S(1)}, u32[]{:S(2)}) %copy-start.1) | copy-done | bytes 20504
  42.3 0.0 copy-start.2
  42.3 0.6 %copy-done.2 = f32[24,256]{1,0:T(8,128)} copy-done((f32[24,256]{1,0:T(8,128)}, f32[24,256]{1,0:T(8,128)S(1)}, u32[]{:S(2)}) %copy-start.2) | copy-done | bytes 24600
  42.9 1.7 %shard_map.86 = (f32[24,256]{1,0:T(8,128)}, f32[64,80]{1,0:T(8,128)}, f32[16,32,64]{2,1,0:T(8,128)}) custom-call(f32[24,256]{1,0:T(8,128)} %copy-done.2, f32[64,80]{1,0:T(8,128)} %copy-done.1, f32[16,32,64]{2,1,0:T(8,128)} %copy-done), custom_call_target="tpu_custom_call" | custom-call | tf_op jit(solution)/shard_map/pallas_call | solution.py:408
Async XLA Ops:
  41.0 0.7 %copy-start = (f32[16,32,64]{2,1,0:T(8,128)}, f32[16,32,64]{2,1,0:T(8,128)S(1)}, u32[]{:S(2)}) copy-start(f32[16,32,64]{2,1,0:T(8,128)S(1)} %get-tuple-element.11.c_ref) | copy-start | bytes 393220
  41.7 0.6 %copy-start.1 = (f32[64,80]{1,0:T(8,128)}, f32[64,80]{1,0:T(8,128)S(1)}, u32[]{:S(2)}) copy-start(f32[64,80]{1,0:T(8,128)S(1)} %get-tuple-element.10.b_ref) | copy-start | bytes 61444
  42.3 0.6 %copy-start.2 = (f32[24,256]{1,0:T(8,128)}, f32[24,256]{1,0:T(8,128)S(1)}, u32[]{:S(2)}) copy-start(f32[24,256]{1,0:T(8,128)S(1)} %get-tuple-element.9.a_ref) | copy-start | bytes 73732

commit v4 on v3

--- a/solution.py
+++ b/solution.py
@@ -27,11 +27,12 @@
 def kernel(
     tex_count, view_count, rates,
     core_hbm, u_hbm, vt_hbm, mask_hbm, lightt_hbm, meas_hbm,
-    u_out, vt_out, core_out,
-    core_ref, u_ref, vt_ref, mask_ref, lightt_ref, usib, uturn,
-    gl, gbuf, meas, mwide, mturn, weights, vcol, vrow, bdw, qbuf, rbuf, p3, pall,
-    ysend, yrecv, ysum, yflat, ytot, ysib, us, ur, gvs, gvr, xs, xr, held, zs, zr,
-    in_sem, w_s, w_r, ga_s, gb_s, gc_s, g_r, p_s, p_r, y_s, y_r, u_s, u_r, gv_s, gv_r,
+    u_hbm_out, vt_hbm_out, core_hbm_out,
+    u_out, vt_out, core_out, out_sem,
+    core_ref, u_ref, vt_ref, mask_ref, lightt_ref, usib, uturn, uown,
+    gl, gbuf, meas, mwide, mturn, weights, vcol, vrow, bdw, qbuf, rbuf, psend, psib, p3, pall,
+    ysend, yrecv, ysum, yflat, ytot, ysib, us, ubuf, gvs, gvr, xs, xr, held, zs, zr,
+    in_sem, w_s, w_r, ga_s, gb_s, g_r, q_s, q_r, p_s, p_r, y_s, y_r, u_s, u_r, gv_s, gv_r,
     h_s, h_r, x_s, x_r, z_s, z_r,
 ):
     na = LINE
@@ -80,7 +81,7 @@
     peers = [(slot(ahead(d), b, core), view) for d in range(1, na)]
     peers += [(slot(a, beside(e), core), view) for e in range(1, nb)]
     peers += [(sibling, view)]
-    peers += [(me, other(w)) for w in range(1, view_count)]
+    peers += [(tex, other(w)) for w in range(1, view_count) for tex in (me, sibling)]
     for peer in peers:
         pl.semaphore_signal(barrier, inc=1, device_id=peer, device_id_type=MESH)
     fetches = [
@@ -99,32 +100,29 @@
 
     for h in range(CHUNKS):
         for e in range(1, nb):
-            push(gl.at[h], gbuf.at[h, me], gb_s.at[h, 0, e - 1], g_r.at[h, me],
+            push(gl.at[h], gbuf.at[h, a, b], gb_s.at[h, 0, e - 1], g_r.at[h, a, b],
                  slot(a, beside(e), core), view)
         for d in range(1, na):
-            push(gl.at[h], gbuf.at[h, me], ga_s.at[h, d - 1], g_r.at[h, me],
+            push(gl.at[h], gbuf.at[h, a, b], ga_s.at[h, d - 1], g_r.at[h, a, b],
                  slot(ahead(d), b, core), view)
-        push(gl.at[h], gbuf.at[h, me], gc_s.at[h, 0, 0], g_r.at[h, me], sibling, view)
     fetches[1].wait()
     push(u_ref, usib, w_s, w_r, sibling, view)
 
     def from_line(h, d):
-        s = slot(ahead(na - d), b, core)
-        arrived(gbuf.at[h, s], g_r.at[h, s])
+        ad = ahead(na - d)
+        arrived(gbuf.at[h, ad, b], g_r.at[h, ad, b])
         for e in range(1, nb):
-            push(gbuf.at[h, s], gbuf.at[h, s], gb_s.at[h, d, e - 1], g_r.at[h, s],
+            push(gbuf.at[h, ad, b], gbuf.at[h, ad, b], gb_s.at[h, d, e - 1], g_r.at[h, ad, b],
                  slot(a, beside(e), core), view)
-        push(gbuf.at[h, s], gbuf.at[h, s], gc_s.at[h, d, 0], g_r.at[h, s], sibling, view)
 
     def from_across(h):
         for d in range(na):
             for e in range(1, nb):
-                s = slot(ahead(na - d), beside(nb - e), core)
-                arrived(gbuf.at[h, s], g_r.at[h, s])
-                push(gbuf.at[h, s], gbuf.at[h, s], gc_s.at[h, d, e], g_r.at[h, s], sibling, view)
-
-    for h in range(CHUNKS):
-        gbuf[h, me] = gl[h]
+                ad, be = ahead(na - d), beside(nb - e)
+                arrived(gbuf.at[h, ad, be], g_r.at[h, ad, be])
+
+    for h in range(CHUNKS):
+        gbuf[h, a, b] = gl[h]
     bdw[...] = jnp.zeros_like(bdw)
     rbuf[...] = jnp.zeros_like(rbuf)
     for fetch in fetches[2:]:
@@ -137,35 +135,42 @@
     vrow[:, :views] = vt_ref[...]
     weights[...] = jnp.broadcast_to(mask_ref[...].astype(F32), (LIGHTS, views)).T
     mwide[...] = meas[...].astype(F32)
-    turns = -(-texels // (CHUNKS * (na - 1)))
+    turns = texels // (2 * CHUNKS * (na - 1))
     t = 0
     for h in range(CHUNKS):
         for d in range(1, na):
             from_line(h, d)
             for _ in range(turns):
-                if t < texels:
-                    mturn[t] = mwide[:, t, :].T
-                    t += 1
-
-    u_bf = u_ref[...].astype(BF)
+                mturn[t] = mwide[:, t, :].T
+                t += 1
+    while t < texels:
+        mturn[t] = mwide[:, t, :].T
+        t += 1
+
     arrived(usib, w_r)
     turned = jnp.concatenate([u_ref[...], usib[...]], axis=0).T
     for j in range(tex_count):
         uturn[j] = turned[j * rows:(j + 1) * rows]
+    pairs = [(ai, bi) for ai in range(na) for bi in range(nb)]
+    uown[...] = jnp.concatenate([uturn[slot(ai, bi, core)] for ai, bi in pairs], axis=0).T.astype(BF)
+    u_own = uown[...]
 
     def stacked(h):
         if rows % 16 == 0:
-            return gbuf[h].reshape(tex_count * rows, part * RL)
+            return gbuf[h].reshape(len(pairs) * rows, part * RL)
         return jnp.concatenate(
-            [gbuf[h, j].astype(F32) for j in range(tex_count)], axis=0).astype(BF)
-
+            [gbuf[h, ai, bi].astype(F32) for ai, bi in pairs], axis=0).astype(BF)
+
+    kept = []
     for h in range(CHUNKS):
         from_across(h)
-        for ai in range(na):
-            for bi in range(nb):
-                s = slot(ai, bi, 1 - core)
-                arrived(gbuf.at[h, s], g_r.at[h, s])
-        proj = jnp.dot(u_bf, stacked(h), preferred_element_type=F32)
+        proj = jnp.dot(u_own, stacked(h), preferred_element_type=F32)
+        psend[h] = proj[texels:]
+        push(psend.at[h], psib.at[h], q_s.at[h], q_r.at[h], sibling, view)
+        kept.append(proj[:texels])
+    for h in range(CHUNKS):
+        arrived(psib.at[h], q_r.at[h])
+        proj = kept[h] + psib[h]
         for j in range(part):
             p3[h, j] = proj[:, j * RL:(j + 1) * RL]
         for t in range(0, texels, 2):
@@ -218,6 +223,11 @@
         s4 = s_all[k * padded:(k + 1) * padded]
         gv = gv + lax.dot_general(p_group(k), s4, NT, preferred_element_type=F32)
 
+    results = [
+        pltpu.make_async_copy(src, dst, out_sem.at[i]) for i, (src, dst) in enumerate((
+            (u_out, u_hbm_out), (vt_out, vt_hbm_out), (core_out, core_hbm_out)))
+    ]
+
     def gv_start(i, value):
         gvs[i] = value
         partner = me + (1 << i) - 2 * (1 << i) * lax.rem(me // (1 << i), 2)
@@ -230,6 +240,7 @@
             gv_start(i + 1, value)
         else:
             vt_out[...] = vt_ref[...] - rate_view * value[:, :views]
+            results[1].start()
 
     gv_start(0, SCALING * gv)
 
@@ -271,12 +282,17 @@
         if h == 0:
             gv_next(0)
 
-    partial = jnp.zeros((2 * texels, RT), F32)
+    partial = jnp.zeros((2 * texels, RT // 2), F32)
     for h in range(CHUNKS):
         partial = partial + lax.dot_general(yflat[h], stacked(h), NT, preferred_element_type=F32)
-    us[...] = SCALING * partial[:texels]
+    us[0] = SCALING * partial[:texels]
+    us[1] = SCALING * partial[texels:]
+    ubuf[view, core] = us[0]
+    targets = [(1, sibling, view)]
     for w in range(1, view_count):
-        push(us, ur.at[w - 1], u_s.at[w - 1], u_r.at[w - 1], me, other(w))
+        targets += [(0, me, other(w)), (1, sibling, other(w))]
+    for i, (half, tex, vw) in enumerate(targets):
+        push(us.at[half], ubuf.at[view, core], u_s.at[i], u_r.at[view, core], tex, vw)
 
     own = []
     for h in range(CHUNKS):
@@ -294,11 +310,15 @@
             gv_next(h + 1)
     for i in range(CHUNKS + 1, steps):
         gv_next(i)
-    total_u = us[...]
+    arrived(ubuf.at[view, 1 - core], u_r.at[view, 1 - core])
     for w in range(1, view_count):
-        arrived(ur.at[w - 1], u_r.at[w - 1])
-        total_u = total_u + ur[w - 1]
+        for ci in range(2):
+            arrived(ubuf.at[other(w), ci], u_r.at[other(w), ci])
+    halves = [sum(ubuf[w, ci] for w in range(view_count)).T for ci in range(2)]
+    total_u = jnp.concatenate(
+        [halves[j % 2][j // 2 * rows:(j // 2 + 1) * rows] for j in range(tex_count)], axis=0).T
     u_out[...] = u_ref[...] - rate_tex * total_u
+    results[0].start()
     for h in range(CHUNKS):
         block = own[h]
         for d in range(1, na):
@@ -308,8 +328,11 @@
         for j in range(part):
             i = h * part + j
             core_out[:, i, :] = core_ref[:, i, :] - block[:, j * RL:(j + 1) * RL]
+    results[2].start()
     for copy in pending:
         copy.wait_send()
+    for result in results:
+        result.wait()
 
 
 def write_out(a_ref, b_ref, c_ref, a_out, b_out, c_out, sems):
@@ -342,7 +365,6 @@
         RV / (texels_all * L),
         RT * RV * RL / (texels_all * VALID * L),
     )
-    vmem = pl.BlockSpec(memory_space=pltpu.VMEM)
     hbm = pl.BlockSpec(memory_space=pltpu.HBM)
     dma = pltpu.SemaphoreType.DMA
     tex_new, view_new, core_new = pl.pallas_call(
@@ -353,8 +375,12 @@
             jax.ShapeDtypeStruct((rows, band, RL), F32),
         ),
         in_specs=[hbm] * 6,
-        out_specs=(vmem, vmem, vmem),
+        out_specs=(hbm, hbm, hbm),
         scratch_shapes=[
+            pltpu.VMEM((texels, RT), F32),
+            pltpu.VMEM((RV, views), F32),
+            pltpu.VMEM((rows, band, RL), F32),
+            dma((3,)),
             pltpu.VMEM((rows, band, RL), F32),
             pltpu.VMEM((texels, RT), F32),
             pltpu.VMEM((RV, views), F32),
@@ -362,8 +388,9 @@
             pltpu.VMEM((RL, L), BF),
             pltpu.VMEM((texels, RT), F32),
             pltpu.VMEM((tex_count, rows, 2 * texels), F32),
+            pltpu.VMEM((2 * texels, RT // 2), BF),
             pltpu.VMEM((CHUNKS, rows, cut), BF),
-            pltpu.VMEM((CHUNKS, tex_count, rows, cut), BF),
+            pltpu.VMEM((CHUNKS, LINE, nb, rows, cut), BF),
             pltpu.VMEM((L, texels, views), BF),
             pltpu.VMEM((L, texels, views), F32),
             pltpu.VMEM((texels, views, L), F32),
@@ -373,6 +400,8 @@
             pltpu.VMEM((GROUP * RL, GROUP * LIGHTS), BF),
             pltpu.VMEM((groups, padded, GROUP * RL), BF),
             pltpu.VMEM((groups, padded, GROUP * LIGHTS), BF),
+            pltpu.VMEM((CHUNKS, texels, cut), F32),
+            pltpu.VMEM((CHUNKS, texels, cut), F32),
             pltpu.VMEM((CHUNKS, part, texels, RL), F32),
             pltpu.VMEM((CHUNKS, view_count, part, texels * RL), BF),
             pltpu.VMEM((CHUNKS, view_count, part, texels * RL), BF),
@@ -381,8 +410,8 @@
             pltpu.VMEM((CHUNKS, 2 * texels, cut), BF),
             pltpu.VMEM((CHUNKS, part, texels * RL), BF),
             pltpu.VMEM((CHUNKS, part, texels * RL), BF),
-            pltpu.VMEM((texels, RT), F32),
-            pltpu.VMEM((peers, texels, RT), F32),
+            pltpu.VMEM((2, texels, RT // 2), F32),
+            pltpu.VMEM((view_count, 2, texels, RT // 2), F32),
             pltpu.VMEM((steps, RV, padded), F32),
             pltpu.VMEM((steps, RV, padded), F32),
             pltpu.VMEM((CHUNKS, LINE, across, rows, cut), BF),
@@ -390,11 +419,11 @@
             pltpu.VMEM((CHUNKS, LINE, rows, cut), F32),
             pltpu.VMEM((CHUNKS, LINE - 1, rows, cut), BF),
             pltpu.VMEM((CHUNKS, LINE - 1, rows, cut), BF),
-            dma((6,)), dma, dma, dma((CHUNKS, LINE - 1)), dma((CHUNKS, LINE, across)), dma((CHUNKS, LINE, nb)),
-            dma((CHUNKS, tex_count)),
+            dma((6,)), dma, dma, dma((CHUNKS, LINE - 1)), dma((CHUNKS, LINE, across)),
+            dma((CHUNKS, LINE, nb)), dma((CHUNKS,)), dma((CHUNKS,)),
             dma((CHUNKS, peers)), dma((CHUNKS, view_count)),
             dma((CHUNKS, peers)), dma((CHUNKS, peers)),
-            dma((peers,)), dma((peers,)), dma((steps,)), dma((steps,)),
+            dma((2 * peers + 1,)), dma((view_count, 2)), dma((steps,)), dma((steps,)),
             dma((CHUNKS,)), dma((CHUNKS,)),
             dma((CHUNKS, LINE, across)), dma((CHUNKS, LINE, across)),
             dma((CHUNKS, LINE - 1)), dma((CHUNKS, LINE - 1)),
@@ -412,10 +441,10 @@
             jax.ShapeDtypeStruct((RV, views), F32),
             jax.ShapeDtypeStruct((rows, band, RL), F32),
         ),
-        in_specs=[vmem] * 3,
+        in_specs=[hbm] * 3,
         out_specs=(hbm, hbm, hbm),
         scratch_shapes=[dma((3,))],
-    )(tex_new, view_new, core_new)
+    )(*(pltpu.with_memory_space_constraint(x, pltpu.HBM) for x in (tex_new, view_new, core_new)))
     return tex_new, view_new.T, core_new
 
 

time: 44.8 us -> 54.3 us (1.21)
  Pallas kernels: 42.1 us -> 51.6 us
    pallas_call x1, Pallas kernels: 1.72 us -> 10.8 us  [per_device(): pl.pallas_call(write_out, out_shape=(jax.ShapeDtypeStruct((texels, RT), F...]
where the time goes in v4:
time: 54.3 us; the launch traced here: 54.1 us
  Pallas kernels  51.6 us (95%)
  local copies, waits for them, and re-layouts  1.9 us (3%)
  between operations  0.65 us (1%)
    pallas_call x1, Pallas kernels, per_device(): pl.pallas_call(functools.partial(kernel, tex_count, view_count, rates), o...  40.8 us
    pallas_call x1, Pallas kernels, per_device(): pl.pallas_call(write_out, out_shape=(jax.ShapeDtypeStruct((texels, RT), F...  10.8 us
    unnamed x6, local copies, waits for them, and re-layouts  1.9 us

profile of v4, /device:TPU:0, one launch (start us, length us, event | category | flops | bytes accessed | tf_op | source)
XLA Modules:
  0.0 54.1 jit_solution(2845520488656420150)
XLA Ops:
  0.6 40.8 %shard_map.85 = (f32[24,256]{1,0:T(8,128)S(1)}, f32[64,80]{1,0:T(8,128)S(1)}, f32[16,32,64]{2,1,0:T(8,128)S(1)}) custom-call(f32[16,32,64]{2,1,0:T(8,128)} %core_hbm.1, f32[24,256]{1,0:T(8,128)} %u_hbm.1, f32[64,80]{1,0:T(8,128)} %bitcast.6, s32[1,80]{1,0:T(1,128)} %bitcast.9, bf16[64,151]{1,0:T(8,128)(2,1)} %bitcast.7, bf16[151,24,80]{2,1,0:T(8,128)(2,1)} %bitcast.5), custom_call_target="tpu_custom_call" | custom-call | flops 1000000000 | bytes 10000000 | tf_op jit(solution)/shard_map/pallas_call | solution.py:370
  41.4 0.0 copy-start
  41.4 0.7 %copy-done = f32[16,32,64]{2,1,0:T(8,128)} copy-done((f32[16,32,64]{2,1,0:T(8,128)}, f32[16,32,64]{2,1,0:T(8,128)S(1)}, u32[]{:S(2)}) %copy-start) | copy-done | bytes 131096
  42.1 0.0 copy-start.1
  42.1 0.6 %copy-done.1 = f32[64,80]{1,0:T(8,128)} copy-done((f32[64,80]{1,0:T(8,128)}, f32[64,80]{1,0:T(8,128)S(1)}, u32[]{:S(2)}) %copy-start.1) | copy-done | bytes 20504
  42.7 0.0 copy-start.2
  42.7 0.6 %copy-done.2 = f32[24,256]{1,0:T(8,128)} copy-done((f32[24,256]{1,0:T(8,128)}, f32[24,256]{1,0:T(8,128)S(1)}, u32[]{:S(2)}) %copy-start.2) | copy-done | bytes 24600
  43.3 10.8 %shard_map.86 = (f32[24,256]{1,0:T(8,128)}, f32[64,80]{1,0:T(8,128)}, f32[16,32,64]{2,1,0:T(8,128)}) custom-call(f32[24,256]{1,0:T(8,128)} %copy-done.2, f32[64,80]{1,0:T(8,128)} %copy-done.1, f32[16,32,64]{2,1,0:T(8,128)} %copy-done), custom_call_target="tpu_custom_call" | custom-call | tf_op jit(solution)/shard_map/pallas_call | solution.py:437
Async XLA Ops:
  41.4 0.7 %copy-start = (f32[16,32,64]{2,1,0:T(8,128)}, f32[16,32,64]{2,1,0:T(8,128)S(1)}, u32[]{:S(2)}) copy-start(f32[16,32,64]{2,1,0:T(8,128)S(1)} %get-tuple-element.11.c_ref) | copy-start | bytes 393220
  42.1 0.6 %copy-start.1 = (f32[64,80]{1,0:T(8,128)}, f32[64,80]{1,0:T(8,128)S(1)}, u32[]{:S(2)}) copy-start(f32[64,80]{1,0:T(8,128)S(1)} %get-tuple-element.10.b_ref) | copy-start | bytes 61444
  42.7 0.6 %copy-start.2 = (f32[24,256]{1,0:T(8,128)}, f32[24,256]{1,0:T(8,128)S(1)}, u32[]{:S(2)}) copy-start(f32[24,256]{1,0:T(8,128)S(1)} %get-tuple-element.9.a_ref) | copy-start | bytes 73732

commit v5 on v4

--- a/solution.py
+++ b/solution.py
@@ -27,8 +27,7 @@
 def kernel(
     tex_count, view_count, rates,
     core_hbm, u_hbm, vt_hbm, mask_hbm, lightt_hbm, meas_hbm,
-    u_hbm_out, vt_hbm_out, core_hbm_out,
-    u_out, vt_out, core_out, out_sem,
+    u_out, vt_out, core_out,
     core_ref, u_ref, vt_ref, mask_ref, lightt_ref, usib, uturn, uown,
     gl, gbuf, meas, mwide, mturn, weights, vcol, vrow, bdw, qbuf, rbuf, psend, psib, p3, pall,
     ysend, yrecv, ysum, yflat, ytot, ysib, us, ubuf, gvs, gvr, xs, xr, held, zs, zr,
@@ -42,8 +41,9 @@
     core = lax.rem(me, 2)
     b = lax.rem(me // 2, nb)
     a = me // (2 * nb)
-    rows, band, _ = core_ref.shape
-    part = band // CHUNKS
+    _, rows, cut = gl.shape
+    part = cut // RL
+    band = part * CHUNKS
     texels = u_ref.shape[0]
     views = vt_ref.shape[1]
     padded = vcol.shape[0]
@@ -93,7 +93,8 @@
         fetch.start()
     fetches[0].wait()
     for i in range(0, band, 2):
-        pair = jnp.concatenate([core_ref[:, i, :], core_ref[:, i + 1, :]], axis=1).astype(BF)
+        pair = jnp.concatenate(
+            [core_ref[pl.ds(i + k, rows, stride=band), :] for k in range(2)], axis=1).astype(BF)
         h, o = divmod(i, part)
         gl[h, :, o * RL:(o + 2) * RL] = pair
     pl.semaphore_wait(barrier, len(peers))
@@ -134,17 +135,17 @@
     vcol[:views, :] = vt_ref[...].T
     vrow[:, :views] = vt_ref[...]
     weights[...] = jnp.broadcast_to(mask_ref[...].astype(F32), (LIGHTS, views)).T
-    mwide[...] = meas[...].astype(F32)
+    mwide[...] = meas[...].astype(F32).reshape(mwide.shape)
     turns = texels // (2 * CHUNKS * (na - 1))
     t = 0
     for h in range(CHUNKS):
         for d in range(1, na):
             from_line(h, d)
             for _ in range(turns):
-                mturn[t] = mwide[:, t, :].T
+                mturn[t] = mwide[pl.ds(t, L, stride=texels), :].T
                 t += 1
     while t < texels:
-        mturn[t] = mwide[:, t, :].T
+        mturn[t] = mwide[pl.ds(t, L, stride=texels), :].T
         t += 1
 
     arrived(usib, w_r)
@@ -172,9 +173,10 @@
         arrived(psib.at[h], q_r.at[h])
         proj = kept[h] + psib[h]
         for j in range(part):
-            p3[h, j] = proj[:, j * RL:(j + 1) * RL]
+            p3[h, j * texels:(j + 1) * texels, :] = proj[:, j * RL:(j + 1) * RL]
         for t in range(0, texels, 2):
-            pair = jnp.concatenate([p3[h, :, t, :], p3[h, :, t + 1, :]], axis=1)
+            pair = jnp.concatenate(
+                [p3[h, pl.ds(t + k, part, stride=texels), :] for k in range(2)], axis=1)
             pall[h, view, :, t * RL:(t + 2) * RL] = pair.astype(BF)
         for w in range(1, view_count):
             push(pall.at[h, view], pall.at[h, view], p_s.at[h, w - 1], p_r.at[h, view],
@@ -223,11 +225,6 @@
         s4 = s_all[k * padded:(k + 1) * padded]
         gv = gv + lax.dot_general(p_group(k), s4, NT, preferred_element_type=F32)
 
-    results = [
-        pltpu.make_async_copy(src, dst, out_sem.at[i]) for i, (src, dst) in enumerate((
-            (u_out, u_hbm_out), (vt_out, vt_hbm_out), (core_out, core_hbm_out)))
-    ]
-
     def gv_start(i, value):
         gvs[i] = value
         partner = me + (1 << i) - 2 * (1 << i) * lax.rem(me // (1 << i), 2)
@@ -240,7 +237,6 @@
             gv_start(i + 1, value)
         else:
             vt_out[...] = vt_ref[...] - rate_view * value[:, :views]
-            results[1].start()
 
     gv_start(0, SCALING * gv)
 
@@ -248,7 +244,7 @@
 
     def turn(h, first, values):
         for t in range(texels):
-            ysum[h, :, first + t, :] = values[:, t * RL:(t + 1) * RL]
+            ysum[h, pl.ds(first + t, part, stride=2 * texels), :] = values[:, t * RL:(t + 1) * RL]
 
     for h in range(CHUNKS):
         total = ysend[h, view].astype(F32)
@@ -268,7 +264,8 @@
         arrived(ysib.at[h], h_r.at[h])
         turn(h, texels, ysib[h].astype(F32))
         for j in range(0, part, 2):
-            pair = jnp.concatenate([ysum[h, j], ysum[h, j + 1]], axis=1)
+            pair = jnp.concatenate(
+                [ysum[h, 2 * texels * k:2 * texels * (k + 1), :] for k in (j, j + 1)], axis=1)
             yflat[h, :, j * RL:(j + 2) * RL] = pair.astype(BF)
         for e in range(1, nb):
             grad = SCALING * jnp.dot(u_parts[e], yflat[h], preferred_element_type=F32)
@@ -318,7 +315,6 @@
     total_u = jnp.concatenate(
         [halves[j % 2][j // 2 * rows:(j // 2 + 1) * rows] for j in range(tex_count)], axis=0).T
     u_out[...] = u_ref[...] - rate_tex * total_u
-    results[0].start()
     for h in range(CHUNKS):
         block = own[h]
         for d in range(1, na):
@@ -327,23 +323,10 @@
         block = rate_core * block
         for j in range(part):
             i = h * part + j
-            core_out[:, i, :] = core_ref[:, i, :] - block[:, j * RL:(j + 1) * RL]
-    results[2].start()
+            at = pl.ds(i, rows, stride=band)
+            core_out[at, :] = core_ref[at, :] - block[:, j * RL:(j + 1) * RL]
     for copy in pending:
         copy.wait_send()
-    for result in results:
-        result.wait()
-
-
-def write_out(a_ref, b_ref, c_ref, a_out, b_out, c_out, sems):
-    copies = [
-        pltpu.make_async_copy(src, dst, sems.at[i])
-        for i, (src, dst) in enumerate(((c_ref, c_out), (a_ref, a_out), (b_ref, b_out)))
-    ]
-    for copy in copies:
-        copy.start()
-    for copy in copies:
-        copy.wait()
 
 
 def per_device(measured, view_mask, tex_factor, view_factor, light_factor, core_tensor):
@@ -365,6 +348,7 @@
         RV / (texels_all * L),
         RT * RV * RL / (texels_all * VALID * L),
     )
+    vmem = pl.BlockSpec(memory_space=pltpu.VMEM)
     hbm = pl.BlockSpec(memory_space=pltpu.HBM)
     dma = pltpu.SemaphoreType.DMA
     tex_new, view_new, core_new = pl.pallas_call(
@@ -372,16 +356,12 @@
         out_shape=(
             jax.ShapeDtypeStruct((texels, RT), F32),
             jax.ShapeDtypeStruct((RV, views), F32),
-            jax.ShapeDtypeStruct((rows, band, RL), F32),
+            jax.ShapeDtypeStruct((rows * band, RL), F32),
         ),
         in_specs=[hbm] * 6,
-        out_specs=(hbm, hbm, hbm),
+        out_specs=(vmem, vmem, vmem),
         scratch_shapes=[
-            pltpu.VMEM((texels, RT), F32),
-            pltpu.VMEM((RV, views), F32),
-            pltpu.VMEM((rows, band, RL), F32),
-            dma((3,)),
-            pltpu.VMEM((rows, band, RL), F32),
+            pltpu.VMEM((rows * band, RL), F32),
             pltpu.VMEM((texels, RT), F32),
             pltpu.VMEM((RV, views), F32),
             pltpu.VMEM((1, views), jnp.int32),
@@ -392,7 +372,7 @@
             pltpu.VMEM((CHUNKS, rows, cut), BF),
             pltpu.VMEM((CHUNKS, LINE, nb, rows, cut), BF),
             pltpu.VMEM((L, texels, views), BF),
-            pltpu.VMEM((L, texels, views), F32),
+            pltpu.VMEM((L * texels, views), F32),
             pltpu.VMEM((texels, views, L), F32),
             pltpu.VMEM((views, LIGHTS), F32),
             pltpu.VMEM((padded, RV), F32),
@@ -402,11 +382,11 @@
             pltpu.VMEM((groups, padded, GROUP * LIGHTS), BF),
             pltpu.VMEM((CHUNKS, texels, cut), F32),
             pltpu.VMEM((CHUNKS, texels, cut), F32),
-            pltpu.VMEM((CHUNKS, part, texels, RL), F32),
+            pltpu.VMEM((CHUNKS, part * texels, RL), F32),
             pltpu.VMEM((CHUNKS, view_count, part, texels * RL), BF),
             pltpu.VMEM((CHUNKS, view_count, part, texels * RL), BF),
             pltpu.VMEM((CHUNKS, peers, part, texels * RL), BF),
-            pltpu.VMEM((CHUNKS, part, 2 * texels, RL), F32),
+            pltpu.VMEM((CHUNKS, part * 2 * texels, RL), F32),
             pltpu.VMEM((CHUNKS, 2 * texels, cut), BF),
             pltpu.VMEM((CHUNKS, part, texels * RL), BF),
             pltpu.VMEM((CHUNKS, part, texels * RL), BF),
@@ -432,20 +412,9 @@
             collective_id=0, has_side_effects=True, vmem_limit_bytes=48 * 1024 * 1024),
         cost_estimate=pl.CostEstimate(flops=10**9, bytes_accessed=10**7, transcendentals=0),
     )(*(pltpu.with_memory_space_constraint(x, pltpu.HBM) for x in (
-        core_tensor, tex_factor, view_factor.T, view_mask.reshape(1, views), light_factor.T,
+        core_tensor.reshape(rows * band, RL), tex_factor, view_factor.T, view_mask.reshape(1, views), light_factor.T,
         jnp.transpose(measured, (2, 0, 1)))))
-    tex_new, view_new, core_new = pl.pallas_call(
-        write_out,
-        out_shape=(
-            jax.ShapeDtypeStruct((texels, RT), F32),
-            jax.ShapeDtypeStruct((RV, views), F32),
-            jax.ShapeDtypeStruct((rows, band, RL), F32),
-        ),
-        in_specs=[hbm] * 3,
-        out_specs=(hbm, hbm, hbm),
-        scratch_shapes=[dma((3,))],
-    )(*(pltpu.with_memory_space_constraint(x, pltpu.HBM) for x in (tex_new, view_new, core_new)))
-    return tex_new, view_new.T, core_new
+    return tex_new, view_new.T, core_new.reshape(core_tensor.shape)
 
 
 def solution(mesh):

time: 54.3 us -> 43.3 us (0.80)
  Pallas kernels: 51.6 us -> 40.5 us
    pallas_call x1 -> x0, Pallas kernels: 10.8 us -> none  [per_device(): pl.pallas_call(write_out, out_shape=(jax.ShapeDtypeStruct((texels, RT), F...]
    unnamed x6 -> x3, local copies, waits for them, and re-layouts: 1.9 us -> 1.93 us
where the time goes in v5:
time: 43.3 us; the launch traced here: 43.1 us
  Pallas kernels  40.5 us (94%)
  local copies, waits for them, and re-layouts  1.93 us (4%)
  between operations  0.64 us (1%)
    pallas_call x1, Pallas kernels, per_device(): pl.pallas_call(functools.partial(kernel, tex_count, view_count, rates), o...  40.5 us
    unnamed x3, local copies, waits for them, and re-layouts  1.93 us

profile of v5, /device:TPU:0, one launch (start us, length us, event | category | flops | bytes accessed | tf_op | source)
XLA Modules:
  0.0 43.1 jit_solution(17153969489562224740)
XLA Ops:
  0.6 40.5 %shard_map.85 = (f32[24,256]{1,0:T(8,128)S(1)}, f32[64,80]{1,0:T(8,128)S(1)}, f32[512,64]{1,0:T(8,128)S(1)}) custom-call(f32[512,64]{1,0:T(8,128)} %bitcast.10, f32[24,256]{1,0:T(8,128)} %u_hbm.1, f32[64,80]{1,0:T(8,128)} %bitcast.11, s32[1,80]{1,0:T(1,128)} %bitcast.13, bf16[64,151]{1,0:T(8,128)(2,1)} %bitcast.12, bf16[151,24,80]{2,1,0:T(8,128)(2,1)} %bitcast.9), custom_call_target="tpu_custom_call" | custom-call | flops 1000000000 | bytes 10000000 | tf_op jit(solution)/shard_map/pallas_call | solution.py:354
  41.2 0.6 %copy.12 = f32[24,256]{1,0:T(8,128)} copy(f32[24,256]{1,0:T(8,128)S(1)} %get-tuple-element.12) | data formatting | bytes 49152
  41.8 0.6 %copy.13 = f32[80,64]{0,1:T(8,128)} copy(f32[80,64]{0,1:T(8,128)S(1)} %bitcast.8) | data formatting | bytes 40960
  42.4 0.7 %copy.14 = f32[16,32,64]{2,1,0:T(8,128)} copy(f32[16,32,64]{2,1,0:T(8,128)S(1)} %bitcast.7) | data formatting | bytes 262144

commit v6 on v5

--- a/solution.py
+++ b/solution.py
@@ -163,13 +163,15 @@
             [gbuf[h, ai, bi].astype(F32) for ai, bi in pairs], axis=0).astype(BF)
 
     kept = []
-    for h in range(CHUNKS):
+
+    def project(h):
         from_across(h)
         proj = jnp.dot(u_own, stacked(h), preferred_element_type=F32)
         psend[h] = proj[texels:]
         push(psend.at[h], psib.at[h], q_s.at[h], q_r.at[h], sibling, view)
         kept.append(proj[:texels])
-    for h in range(CHUNKS):
+
+    def exchange(h):
         arrived(psib.at[h], q_r.at[h])
         proj = kept[h] + psib[h]
         for j in range(part):
@@ -181,6 +183,12 @@
         for w in range(1, view_count):
             push(pall.at[h, view], pall.at[h, view], p_s.at[h, w - 1], p_r.at[h, view],
                  me, other(w))
+
+    project(0)
+    for h in range(1, CHUNKS):
+        exchange(h - 1)
+        project(h)
+    exchange(CHUNKS - 1)
     v_bf = vcol[...].astype(BF)
     vt_bf = vrow[...].astype(BF)
     for h in range(CHUNKS):
@@ -246,7 +254,7 @@
         for t in range(texels):
             ysum[h, pl.ds(first + t, part, stride=2 * texels), :] = values[:, t * RL:(t + 1) * RL]
 
-    for h in range(CHUNKS):
+    def add_views(h):
         total = ysend[h, view].astype(F32)
         for w in range(1, view_count):
             arrived(yrecv.at[h, w - 1], y_r.at[h, w - 1])
@@ -260,6 +268,7 @@
             [uturn[slot(ahead(d), beside(e), core)] for d in order], axis=0).astype(BF)
 
     u_parts = [u_rows(e) for e in range(nb)]
+    add_views(0)
     for h in range(CHUNKS):
         arrived(ysib.at[h], h_r.at[h])
         turn(h, texels, ysib[h].astype(F32))
@@ -276,6 +285,8 @@
         grad = SCALING * jnp.dot(u_parts[0], yflat[h], preferred_element_type=F32)
         for i, d in enumerate(order):
             held[h, d] = grad[i * rows:(i + 1) * rows]
+        if h + 1 < CHUNKS:
+            add_views(h + 1)
         if h == 0:
             gv_next(0)
 

time: 43.3 us -> 43 us (level)
  no operation moved by 1% of the time
where the time goes in v6:
time: 43 us; the launch traced here: 42.8 us
  Pallas kernels  40.3 us (94%)
  local copies, waits for them, and re-layouts  1.93 us (4%)
  between operations  0.64 us (1%)
    pallas_call x1, Pallas kernels, per_device(): pl.pallas_call(functools.partial(kernel, tex_count, view_count, rates), o...  40.3 us
    unnamed x3, local copies, waits for them, and re-layouts  1.93 us

profile of v6, /device:TPU:0, one launch (start us, length us, event | category | flops | bytes accessed | tf_op | source)
XLA Modules:
  0.0 42.8 jit_solution(4846382221287903177)
XLA Ops:
  0.6 40.3 %shard_map.85 = (f32[24,256]{1,0:T(8,128)S(1)}, f32[64,80]{1,0:T(8,128)S(1)}, f32[512,64]{1,0:T(8,128)S(1)}) custom-call(f32[512,64]{1,0:T(8,128)} %bitcast.10, f32[24,256]{1,0:T(8,128)} %u_hbm.1, f32[64,80]{1,0:T(8,128)} %bitcast.11, s32[1,80]{1,0:T(1,128)} %bitcast.13, bf16[64,151]{1,0:T(8,128)(2,1)} %bitcast.12, bf16[151,24,80]{2,1,0:T(8,128)(2,1)} %bitcast.9), custom_call_target="tpu_custom_call" | custom-call | flops 1000000000 | bytes 10000000 | tf_op jit(solution)/shard_map/pallas_call | solution.py:365
  40.9 0.6 %copy.12 = f32[24,256]{1,0:T(8,128)} copy(f32[24,256]{1,0:T(8,128)S(1)} %get-tuple-element.12) | data formatting | bytes 49152
  41.5 0.6 %copy.13 = f32[80,64]{0,1:T(8,128)} copy(f32[80,64]{0,1:T(8,128)S(1)} %bitcast.8) | data formatting | bytes 40960
  42.1 0.7 %copy.14 = f32[16,32,64]{2,1,0:T(8,128)} copy(f32[16,32,64]{2,1,0:T(8,128)S(1)} %bitcast.7) | data formatting | bytes 262144

commit v7 on v6

--- a/solution.py
+++ b/solution.py
@@ -136,17 +136,18 @@
     vrow[:, :views] = vt_ref[...]
     weights[...] = jnp.broadcast_to(mask_ref[...].astype(F32), (LIGHTS, views)).T
     mwide[...] = meas[...].astype(F32).reshape(mwide.shape)
+    waiting = list(range(texels))
+
+    def turn_measured(count):
+        for _ in range(min(count, len(waiting))):
+            t = waiting.pop(0)
+            mturn[t] = mwide[pl.ds(t, L, stride=texels), :].T
+
     turns = texels // (2 * CHUNKS * (na - 1))
-    t = 0
     for h in range(CHUNKS):
         for d in range(1, na):
             from_line(h, d)
-            for _ in range(turns):
-                mturn[t] = mwide[pl.ds(t, L, stride=texels), :].T
-                t += 1
-    while t < texels:
-        mturn[t] = mwide[pl.ds(t, L, stride=texels), :].T
-        t += 1
+            turn_measured(turns)
 
     arrived(usib, w_r)
     turned = jnp.concatenate([u_ref[...], usib[...]], axis=0).T
@@ -186,9 +187,12 @@
 
     project(0)
     for h in range(1, CHUNKS):
+        turn_measured(turns * 2)
         exchange(h - 1)
         project(h)
+    turn_measured(turns * 2)
     exchange(CHUNKS - 1)
+    turn_measured(texels)
     v_bf = vcol[...].astype(BF)
     vt_bf = vrow[...].astype(BF)
     for h in range(CHUNKS):

time: 43 us -> 43 us (level)
  no operation moved by 1% of the time
where the time goes in v7:
time: 43 us; the launch traced here: 42.8 us
  Pallas kernels  40.3 us (94%)
  local copies, waits for them, and re-layouts  1.93 us (4%)
  between operations  0.64 us (1%)
    pallas_call x1, Pallas kernels, per_device(): pl.pallas_call(functools.partial(kernel, tex_count, view_count, rates), o...  40.3 us
    unnamed x3, local copies, waits for them, and re-layouts  1.93 us

profile of v7, /device:TPU:0, one launch (start us, length us, event | category | flops | bytes accessed | tf_op | source)
XLA Modules:
  0.0 42.8 jit_solution(12516414243407142069)
XLA Ops:
  0.6 40.3 %shard_map.85 = (f32[24,256]{1,0:T(8,128)S(1)}, f32[64,80]{1,0:T(8,128)S(1)}, f32[512,64]{1,0:T(8,128)S(1)}) custom-call(f32[512,64]{1,0:T(8,128)} %bitcast.10, f32[24,256]{1,0:T(8,128)} %u_hbm.1, f32[64,80]{1,0:T(8,128)} %bitcast.11, s32[1,80]{1,0:T(1,128)} %bitcast.13, bf16[64,151]{1,0:T(8,128)(2,1)} %bitcast.12, bf16[151,24,80]{2,1,0:T(8,128)(2,1)} %bitcast.9), custom_call_target="tpu_custom_call" | custom-call | flops 1000000000 | bytes 10000000 | tf_op jit(solution)/shard_map/pallas_call | solution.py:369
  40.9 0.6 %copy.12 = f32[24,256]{1,0:T(8,128)} copy(f32[24,256]{1,0:T(8,128)S(1)} %get-tuple-element.12) | data formatting | bytes 49152
  41.5 0.6 %copy.13 = f32[80,64]{0,1:T(8,128)} copy(f32[80,64]{0,1:T(8,128)S(1)} %bitcast.8) | data formatting | bytes 40960
  42.1 0.7 %copy.14 = f32[16,32,64]{2,1,0:T(8,128)} copy(f32[16,32,64]{2,1,0:T(8,128)S(1)} %bitcast.7) | data formatting | bytes 262144
